TPU v7x, 32 devices: a whole 2x2x4 slice. The times are simulated.
32 devices in a mesh: dp: 16 (over z, x, core), blk: 2 (over y).
Axes of the slice: x: 2, y: 2, z: 4, core: 2. Of those that a mesh axis runs over, the one named last changes fastest.
Arguments:
- tokens: bfloat16 [16, 768, 768], P('dp', 'blk'), may hold values from -6 to 6
- visible: int32 [16, 768], P('dp', 'blk'), may hold values from 0 to 1535, as said below
- ln1_gain: float32 [768], replicated, may hold values from 0.1 to 1.9
- w_qkv: bfloat16 [768, 2304], replicated, may hold values from -0.21875 to 0.21875
- w_proj: bfloat16 [768, 768], replicated, may hold values from -3.5 to 3.5
- ln2_gain: float32 [768], replicated, may hold values from 0.1 to 1.9
- w_up: bfloat16 [768, 3072], replicated, may hold values from -0.21875 to 0.21875
- w_down: bfloat16 [3072, 768], replicated, may hold values from -0.109375 to 0.109375
- d_out: bfloat16 [16, 768, 768], P('dp', 'blk'), may hold values from -6 to 6
Outputs:
- out: bfloat16 [16, 768, 768], P('dp', 'blk')
- d_tokens: float32 [16, 768, 768], P('dp', 'blk')
- d_ln1_gain: float32 [768], replicated
- d_w_qkv: float32 [768, 2304], replicated
- d_w_proj: float32 [768, 768], replicated
- d_ln2_gain: float32 [768], replicated
- d_w_up: float32 [768, 3072], replicated
- d_w_down: float32 [3072, 768], replicated
Inputs may be any that keep to these rules, and one draw needn't show every extreme that they name: `visible`: each row is strictly increasing, starts at 0 and ends at 1535.
All inputs are finite; a program needn't handle non-finite values.
Results may differ from a plain program's by a relative error of at most 0.015.
Values may be sent and summed in bfloat16 or wider, within the bound.
No kernel may reach another device: no remote copies, remote signals or barrier semaphores. Data moves between devices by JAX's collectives and lax.ppermute only.
A program may use at most 192 MiB of HBM per device.

v0:
```python
import functools
import math

import jax
import jax.numpy as jnp
from jax import lax
from jax.experimental import pallas as pl
from jax.experimental.pallas import tpu as pltpu
from jax.sharding import PartitionSpec as P

HEADS = 12
HD = 64
PAIR = 2 * HD
GROUP = 2
BACK_GROUP = 1
BACK_LIMIT = 28
epsilon = 1e-06
f32 = jnp.float32
bf16 = jnp.bfloat16
NN = ((1,), (0,))
NT = ((1,), (1,))
TN = ((0,), (0,))
AXES = ("dp", "blk")
MIB = 1 << 20


def dot(left, right, dims=NN):
    return lax.dot_general(left, right, (dims, ((), ())), preferred_element_type=f32)


def position_table(visible, width):
    half = width // 2
    column = jnp.arange(half, dtype=f32)
    freqs = jnp.exp(column * (-math.log(10000.0) / half))
    angles = visible.astype(f32)[..., None] * freqs
    return jnp.concatenate([jnp.sin(angles), jnp.cos(angles)], -1)


def normalize(values):
    center = values - jnp.mean(values, -1, keepdims=True)
    spread = jnp.mean(center * center, -1, keepdims=True)
    scale = lax.rsqrt(spread + epsilon)
    return center * scale, scale


def norm_backward(grad, gain, xhat, scale):
    e = grad * gain
    return scale * (
        e - jnp.mean(e, -1, keepdims=True) - xhat * jnp.mean(e * xhat, -1, keepdims=True)
    )


def call(kernel, grid, in_specs, out_specs, out_shape, args, scalars, vmem, scratch=(), aliases=None):
    return pl.pallas_call(
        kernel,
        grid_spec=pltpu.PrefetchScalarGridSpec(
            num_scalar_prefetch=1,
            grid=grid,
            in_specs=in_specs,
            out_specs=out_specs,
            scratch_shapes=list(scratch),
        ),
        out_shape=out_shape,
        input_output_aliases=aliases or {},
        compiler_params=pltpu.CompilerParams(vmem_limit_bytes=max(vmem, 28) * MIB),
        cost_estimate=pl.CostEstimate(flops=1, bytes_accessed=1, transcendentals=0),
    )(scalars, *args)


def spec(shape, index):
    return pl.BlockSpec(shape, index)


def whole(array):
    zeros = (0,) * array.ndim
    return pl.BlockSpec(array.shape, lambda i, s: zeros)


def shape(dims, dtype):
    return jax.ShapeDtypeStruct(dims, dtype)


FF_ORDERS = (
    (("x", "y", "z0", "z1"), ("y", "z0", "x", "z1")),
    (("z0", "y", "x", "z1"), ("x", "y", "z1", "z0")),
    (("y", "z0", "x", "z1"), ("x", "y", "z0", "z1")),
)
QKV_ORDER = (("x", "z0", "z1"), ("z0", "z1", "x"))
PLAN = (
    ("ff", 0), ("wait", "early"), ("ff", 1), ("wait", "e0"), ("dw", 0), ("own",),
    ("wait", "branch_other"), ("wait", "e2"), ("wait", "g"), ("dw", 2), ("wait", "e1"), ("dw", 1),
    ("go", 0), ("far",), ("go", 2), ("joint",), ("go", 0), ("go", 2), ("go", 1), ("go", 0),
    ("go", 3), ("go", 2), ("back",), ("go", 3), ("go", 1), ("go", 0), ("wait", "bf"), ("go", 2),
    ("go", 0), ("go", 3), ("go", 2), ("go", 1), ("go", 3), ("go", 0), ("go", 3), ("go", 2),
    ("go", 1), ("wait", "n0"), ("go", 0), ("unpack", 0, 0), ("go", 3), ("go", 1), ("wait", "f0"),
    ("tokens",), ("unpack", 0, 1), ("go", 2), ("wait", "n2"), ("unpack", 2, 0), ("go", 1),
    ("go", 3), ("wait", "f2"), ("wait", "n3"), ("unpack", 2, 1), ("unpack", 3, 0), ("wait", "f3"),
    ("unpack", 3, 1), ("go", 1), ("wait", "n1"), ("unpack", 1, 0), ("wait", "f1"), ("unpack", 1, 1),
)
DP_BIT = {"c": 1, "x": 2, "z0": 4, "z1": 8}


def swap(array, first, second=None):
    second = second or first
    pairs = []
    for d in range(16):
        for b in range(2):
            bit = second if d & 1 else first
            to = (d, b ^ 1) if bit == "y" else (d ^ DP_BIT[bit], b)
            pairs.append((d * 2 + b, to[0] * 2 + to[1]))
    return lax.ppermute(array, AXES, pairs)


def place(order):
    d, b = lax.axis_index("dp"), lax.axis_index("blk")
    code = jnp.int32(0)
    for bit in order:
        value = b & 1 if bit == "y" else (d // DP_BIT[bit]) & 1
        code = code * 2 + value
    return code


def places(orders):
    core = lax.axis_index("dp") & 1
    first, second = place(orders[0]), place(orders[1])
    return jnp.where(core == 0, first, second), jnp.where(core == 0, second, first)


def add(a, b):
    return (a.astype(f32) + b.astype(f32)).astype(bf16)


class Order:
    def __init__(self):
        self.last = None

    def pin(self, *arrays):
        if self.last is None:
            return arrays
        return lax.optimization_barrier((*arrays, self.last))[:-1]

    def run(self, function, *arrays):
        result = function(*self.pin(*arrays))
        self.last = result[0] if isinstance(result, (tuple, list)) else result
        return result

    def swap(self, array, first, second=None):
        return swap(self.pin(array)[0], first, second)


def total(order, keep, send, links, widen=None):
    received = order.swap(send, *links[0])
    yield
    for link in links[1:-1]:
        half = keep.shape[0] // 2
        send = order.run(lambda k, r: add(k[half:], r[half:]), keep, received)
        coming = order.swap(send, *link)
        keep = order.run(lambda k, r: add(k[:half], r[:half]), keep, received)
        received = coming
        yield
    keep = order.run(add, keep, received)
    received = order.swap(keep, *links[-1])
    yield
    block = order.run(lambda k, r: add(k, r[::-1]), keep, received)
    if widen is not None:
        received = order.swap(block, "y")
        yield
        block = order.run(widen, block, received)
    back = [link for link in links[:-1] if link[0] != "c"][::-1]
    for link in back[:-1]:
        received = order.swap(block, *link)
        yield
        block = order.run(lambda k, r: jnp.concatenate([k, r], 0), block, received)
    far = order.swap(block, *back[-1])
    other = order.swap(block, "c")
    yield block, other
    far = order.run(lambda value: value, far)
    yield far, order.swap(far, "c")


def sine_and_cosine(angle):
    turns = jnp.floor(angle * (2.0 / math.pi) + 0.5)
    rest = angle - turns * 1.5703125
    rest = rest - turns * 4.837512969970703125e-4
    rest = rest - turns * 7.54978995489188e-8
    square = rest * rest
    sine = rest + rest * square * (
        -1.6666654611e-1 + square * (8.3321608736e-3 + square * -1.9515295891e-4)
    )
    cosine = (1.0 - 0.5 * square) + square * square * (
        4.166664568298827e-2 + square * (-1.388731625493765e-3 + square * 2.443315711809948e-5)
    )
    quarter = turns.astype(jnp.int32)
    odd = (quarter & 1) == 1
    sin = jnp.where(odd, cosine, sine)
    cos = jnp.where(odd, sine, cosine)
    return (
        jnp.where((quarter & 2) == 2, -sin, sin),
        jnp.where(((quarter + 1) & 2) == 2, -cos, cos),
    )


def position_kernel(s, visible, freqs, out):
    column = jnp.broadcast_to(visible[...].astype(f32), (8, visible.shape[1])).T[:, :1]
    sin, cos = sine_and_cosine(column * freqs[...])
    half = sin.shape[1]
    out[:, :half] = sin
    out[:, half:] = cos


def positions(scalars, visible, freqs):
    rows, width = visible.shape[1], 2 * freqs.shape[1]
    out = shape((rows, width), f32)
    return call(
        position_kernel, (1,), [whole(visible), whole(freqs)], whole(out), out, (visible, freqs), scalars, 16
    )


def ln_qkv_kernel(s, tok, pos, gain, w, normed, qkv, *resid):
    @pl.when(pl.program_id(0) == 0)
    def _():
        value = tok[...].astype(f32) + pos[...]
        if resid:
            resid[0][...] = value
        xhat, _ = normalize(value)
        normed[...] = (xhat * gain[...]).astype(bf16)

    qkv[...] = dot(normed[...], w[...]).astype(bf16)


def ln_qkv(scalars, far, tok, pos, gain, w):
    rows, width = tok.shape
    full = spec((rows, width), lambda i, s: (0, 0))
    parts = 2 if far else 3
    out_shape = [shape((rows, width), bf16), shape((rows, parts * width), bf16)]
    return call(
        ln_qkv_kernel,
        (parts,),
        [full, full, whole(gain), spec((width, width), lambda i, s: (0, i + far))],
        [full, spec((rows, width), lambda i, s: (0, i))] + [full] * (not far),
        out_shape + [shape((rows, width), f32)] * (not far),
        (tok, pos, gain, w),
        scalars,
        24,
    )


def far_query_kernel(s, normed, w, out):
    out[...] = dot(normed[...], w[...]).astype(bf16)


def far_query(scalars, normed, w):
    rows, width = normed.shape
    out = shape((rows, width // 2), bf16)
    return call(
        far_query_kernel,
        (1,),
        [whole(normed), spec((width, width // 2), lambda i, s: (0, s[1]))],
        whole(out),
        out,
        (normed, w),
        scalars,
        16,
    )


def head_masks(x):
    lane = lax.broadcasted_iota(jnp.int32, x.shape, 1)
    return jnp.where(lane < HD, x, 0.0).astype(bf16), jnp.where(lane >= HD, x, 0.0).astype(bf16)


def attn_kernel(group, s, q, k, v, *refs):
    rows = q.shape[0]
    later = len(refs) == 3
    if later:
        acc_in, stat_in, out = refs
    else:
        acc, stat = refs
    for pair in range(group):
        lanes = slice(pair * PAIR, (pair + 1) * PAIR)
        qs = jnp.concatenate(head_masks(q[:, lanes].astype(f32) * HD**-0.5), 0)
        scores = dot(k[:, lanes], qs, NT)
        top = jnp.max(scores, 0, keepdims=True)
        if later:
            before = stat_in[pair, 0:1]
            top = jnp.maximum(top, before)
        e = jnp.exp(scores - top)
        total = jnp.sum(e, 0, keepdims=True)
        vt = v[:, lanes].T
        low = e.astype(bf16)
        parts = [dot(vt[h * HD : (h + 1) * HD], low[:, h * rows : (h + 1) * rows]) for h in range(2)]
        if not later:
            acc[pair] = jnp.concatenate(parts, 0)
            stat[pair, 0:1] = top
            stat[pair, 1:2] = total
            continue
        shrink = jnp.exp(before - top)
        scale = 1.0 / (total + stat_in[pair, 1:2] * shrink)
        shrink = shrink * scale
        for h in range(2):
            at = slice(h * rows, (h + 1) * rows)
            held = acc_in[pair, h * HD : (h + 1) * HD]
            parts[h] = parts[h] * scale[:, at] + held * shrink[:, at]
        out[:, lanes] = jnp.concatenate(parts, 0).T.astype(bf16)


def attention(scalars, qkv, keys, *so_far):
    rows, width = qkv.shape[0], qkv.shape[1] // 3
    pairs = width // PAIR
    group = GROUP
    steps = pairs // group

    def column(part):
        return spec((rows, group * PAIR), lambda i, s: (0, part * steps + i))

    first = 0 if so_far else 1
    acc = spec((group, PAIR, rows), lambda i, s: (i, 0, 0))
    stat = spec((group, 8, 2 * rows), lambda i, s: (i, 0, 0))
    sums = [shape((pairs, PAIR, rows), f32), shape((pairs, 8, 2 * rows), f32)]
    return call(
        functools.partial(attn_kernel, group),
        (steps,),
        [column(0), column(first), column(first + 1)] + ([acc, stat] if so_far else []),
        spec((rows, group * PAIR), lambda i, s: (0, i)) if so_far else [acc, stat],
        shape((rows, width), bf16) if so_far else sums,
        (qkv, keys, keys) + so_far,
        scalars,
        28,
    )


def low_rows(packed):
    return packed.shape[0] - packed.shape[1]


def proj_kernel(s, att, att_half, w, resid, gain, resid2, normed2, packed):
    packed[low_rows(packed) :] = att_half[...]
    value = resid[...] + dot(att[...], w[...])
    resid2[...] = value
    xhat, _ = normalize(value)
    low = (xhat * gain[...]).astype(bf16)
    normed2[...] = low
    packed[: low_rows(packed)] = low.T


def project(scalars, att, w, resid, gain):
    rows, width = att.shape
    full = spec((rows, width), lambda i, s: (0, 0))
    half = spec((rows, width // 2), lambda i, s: (0, 1 - s[0]))
    return call(
        proj_kernel,
        (1,),
        [full, half, whole(w), full, whole(gain)],
        [
            full,
            full,
            spec((width + rows, rows), lambda i, s: (0, 0)),
        ],
        [
            shape((rows, width), f32),
            shape((rows, width), bf16),
            shape((width + rows, rows), bf16),
        ],
        (att, att, w, resid, gain),
        scalars,
        24,
    )


def gelu_and_slope(v):
    c = math.sqrt(2.0 / math.pi)
    square = v * v
    t = jnp.tanh(v * (c + (c * 0.044715) * square))
    act = 0.5 * v * (1.0 + t)
    slope = 0.5 * (1.0 + t) + (0.5 * v) * (1.0 - t * t) * (c + (3.0 * c * 0.044715) * square)
    return act, slope


def ff_kernel(count, s, normed, cot, up, down, *refs):
    step = pl.program_id(0)
    if count > 1:
        out_in, back_in, resid2, gain, w_own, w_other, *refs = refs
    pieces, refs = refs[: 2 * count], refs[2 * count :]
    if count > 1:
        out_low, grad2, branch, g_own, g_other, out, back = refs
    else:
        out, back = refs
    hidden = dot(normed[...], up[...])
    act, slope = gelu_and_slope(hidden)
    act = act.astype(bf16)
    grad = (dot(cot[...], down[...], NT) * slope).astype(bf16)
    out_part = dot(act, down[...])
    back_part = dot(grad, up[...], NT)

    @pl.when(step == 0)
    def _():
        out[...] = out_in[...] + out_part if count > 1 else out_part
        back[...] = back_in[...] + back_part if count > 1 else back_part

    @pl.when(step > 0)
    def _():
        out[...] += out_part
        back[...] += back_part

    for at, piece in enumerate(pieces):

        @pl.when(step == at)
        def _(piece=piece):
            piece[0] = act
            piece[1] = grad

    if count > 1:

        @pl.when(step == 2 * count - 1)
        def _():
            value = resid2[...]
            out_low[...] = (value + out[...]).astype(bf16)
            xhat, scale = normalize(value)
            g = cot[...].astype(f32) + norm_backward(back[...], gain[...], xhat, scale)
            grad2[...] = g
            low = g.astype(bf16)
            branch[...] = low
            g_other[...] = dot(low, w_other[...], NT).astype(bf16)
            g_own[...] = dot(low, w_own[...], NT).astype(bf16)


def ff_chunks(scalars, first, count, normed, cot, up, down, *more):
    rows, width = normed.shape
    half = width // 2
    wide = 512

    def column(i, s):
        return 2 * (first + i // 2) + (s[0] ^ (1 - (i & 1)))

    full = spec((rows, width), lambda i, s: (0, 0))
    part = spec((rows, half), lambda i, s: (0, 0))
    in_specs = [
        whole(normed),
        whole(cot),
        spec((width, wide), lambda i, s: (0, column(i, s))),
        spec((wide, width), lambda i, s: (column(i, s), 0)),
    ]
    out_specs = [spec((2, rows, wide), lambda i, s: (0, 0, 0))] * (2 * count)
    out_shape = [shape((2, rows, wide), bf16)] * (2 * count)
    scratch = []
    if count > 1:
        in_specs += [
            full,
            full,
            full,
            spec((1, width), lambda i, s: (0, 0)),
            spec((half, width), lambda i, s: (s[1], 0)),
            spec((half, width), lambda i, s: (1 - s[1], 0)),
        ]
        out_specs += [full, full, full, part, part]
        out_shape += [shape((rows, width), t) for t in (bf16, f32, bf16)]
        out_shape += [shape((rows, half), bf16)] * 2
        scratch = [pltpu.VMEM((rows, width), f32)] * 2
    else:
        out_specs += [full, full]
        out_shape += [shape((rows, width), f32)] * 2
    return call(
        functools.partial(ff_kernel, count),
        (2 * count,),
        in_specs,
        out_specs,
        out_shape,
        (normed, cot, up, down) + more,
        scalars,
        28,
        scratch,
    )


def ff_grads_kernel(at, s, act, act_o, grad, grad_o, cot, cot_o, nt, nt_o, *refs):
    keep, send = refs[-2:]
    step = pl.program_id(0)
    rows_both = jnp.concatenate([cot[...], cot_o[...]], 0)
    g_down = dot(jnp.concatenate([act[0], act_o[0]], 0), rows_both, TN).astype(bf16)
    grads = jnp.concatenate([grad[0], grad_o[0]], 0)
    g_up = dot(jnp.concatenate([nt[...], nt_o[...]], 1), grads).astype(bf16)
    g_proj = None
    if len(refs) > 2:
        att, att_o, branch, branch_o = refs[:4]
        both = jnp.concatenate([branch[...], branch_o[...]], 0)
        g_proj = dot(jnp.concatenate([att[...], att_o[...]], 0), both, TN).astype(bf16)
    code = s[at] & 7

    def store(target):
        rows_d = g_down.shape[0] // 8
        rows_u = g_up.shape[0] // 8
        half = g_up.shape[1] // 2
        for block in range(8):
            to = block ^ code
            target[to, :rows_d, :] = g_down[block * rows_d : (block + 1) * rows_d]
            part = g_up[block * rows_u : (block + 1) * rows_u]
            target[to, 32:64, : 2 * half] = part[:32]
            target[to, 32:48, 2 * half :] = part[32:, :half]
            target[to, 48:64, 2 * half :] = part[32:, half:]
            if g_proj is not None:
                part = g_proj[block * rows_u : (block + 1) * rows_u]
                wide = part.shape[1]
                target[to, 64:80, :wide] = part[:16]
                target[to, 64:80, wide:] = part[16:32]
                target[to, 80:, :wide] = part[32:]
                target[to, 80:, wide:] = jnp.zeros_like(part[32:])

    @pl.when(step == 0)
    def _():
        store(send)

    @pl.when(step == 1)
    def _():
        store(keep)


def ff_grads(scalars, chunk, mine, theirs, cot, cot_other, normed_t_other, normed_t, *proj):
    rows, width = cot.shape
    wide = mine.shape[2]
    at = 2 + 2 * chunk

    def side(i, s):
        return (1 - i) ^ (s[at] // 8)

    act = spec((1, rows, wide // 2), lambda i, s: (0, 0, side(i, s)))
    grad = spec((1, rows, wide), lambda i, s: (1, 0, 0))
    feature = spec((width // 2, rows), lambda i, s: (side(i, s), 0))
    in_specs = [act, act, grad, grad, whole(cot), whole(cot), feature, feature]
    if proj:
        half = width // 2
        column = spec((rows, half), lambda i, s: (0, side(i, s)))
        packed = spec((rows, half), lambda i, s: (2, 0))
        in_specs += [spec((rows, half), lambda i, s: (0, s[0])), packed, column, column]
    deep = 96 if proj else 64
    piece = spec((8, deep, width), lambda i, s: (0, 0, 0))
    return call(
        functools.partial(ff_grads_kernel, at),
        (2,),
        in_specs,
        [piece, piece],
        [shape((8, deep, width), bf16)] * 2,
        (mine, theirs, mine, theirs, cot, cot_other, normed_t, normed_t_other) + proj,
        scalars,
        28,
    )


def attn_back_kernel(group, s, q, g, k_o, k_f, v_o, v_f, *refs):
    gk_in, gv_in = refs[:2] if len(refs) == 5 else (None, None)
    gq, gk, gv = refs[-3:]
    rows = q.shape[0]
    for pair in range(group):
        lanes = slice(pair * PAIR, (pair + 1) * PAIR)
        k = jnp.concatenate([k_o[:, lanes], k_f[:, lanes]], 0)
        v = jnp.concatenate([v_o[:, lanes], v_f[:, lanes]], 0)
        kt = (k.astype(f32) * HD**-0.5).astype(bf16).T
        qs = jnp.concatenate(head_masks(q[:, lanes].astype(f32) * HD**-0.5), 0)
        gs = jnp.concatenate(head_masks(g[:, lanes].astype(f32)), 0)
        scores = dot(k, qs, NT)
        e = jnp.exp(scores - jnp.max(scores, 0, keepdims=True))
        probs = e * (1.0 / jnp.sum(e, 0, keepdims=True))
        grad_v = dot(probs.astype(bf16), gs)
        grad_p = dot(v, gs, NT)
        row = jnp.sum(probs * grad_p, 0, keepdims=True)
        grad_s = (probs * (grad_p - row)).astype(bf16)
        grad_k = dot(grad_s, qs)
        grad_q = [
            dot(kt[h * HD : (h + 1) * HD], grad_s[:, h * rows : (h + 1) * rows]) for h in range(2)
        ]
        if gk_in is not None:
            grad_k, grad_v = grad_k + gk_in[:, lanes], grad_v + gv_in[:, lanes]
        gq[:, lanes] = jnp.concatenate(grad_q, 0).T.astype(bf16)
        gk[:, lanes] = grad_k.astype(gk.dtype)
        gv[:, lanes] = grad_v.astype(gv.dtype)


def attention_back(scalars, query, grad, qkv, kv_far, *so_far):
    rows, width = qkv.shape[0], qkv.shape[1] // 3
    mine = width // PAIR // 2
    group = BACK_GROUP
    steps = mine // group

    def column(part):
        return spec((rows, group * PAIR), lambda i, s: (0, (2 * part + s[1]) * steps + i))

    block = spec((rows, group * PAIR), lambda i, s: (0, i))
    both = spec((2 * rows, group * PAIR), lambda i, s: (0, i))
    dtype = bf16 if so_far else f32
    return call(
        functools.partial(attn_back_kernel, group),
        (steps,),
        [block if so_far else column(0), block, column(1), column(0), column(2), column(1)]
        + [both] * len(so_far),
        [block, both, both],
        [shape((rows, width // 2), bf16)] + [shape((2 * rows, width // 2), dtype)] * 2,
        (query, grad, qkv, kv_far, qkv, kv_far) + so_far,
        scalars,
        BACK_LIMIT,
    )


def joint_kernel(s, n_own, n_far, gq_o, gq_f, gk, gv, keep, send):
    step = pl.program_id(0)
    gq = jnp.concatenate([gq_o[...], gq_f[...]], 0)
    n = jnp.concatenate([n_own[...], n_far[...]], 0)
    cols = gk.shape[1]

    def fill(target, code):
        tiles = [dot(n, g, TN).astype(bf16) for g in (gq, gk[...], gv[...])]
        rows = tiles[0].shape[0] // 8
        for block in range(8):
            at = block ^ code
            for i, tile in enumerate(tiles):
                part = tile[block * rows : (block + 1) * rows]
                target[at, :, i * cols : i * cols + part.shape[1]] = part

    @pl.when(step == 0)
    def _():
        fill(send, s[9])

    @pl.when(step == 1)
    def _():
        fill(keep, s[8])


def joint_grads(scalars, n_own, n_far, gq, gq_far, gk, gv):
    rows, width = n_own.shape
    half = width // 2
    feature = spec((rows, half), lambda i, s: (0, s[0] ^ (1 - i)))
    cols = 3 * half
    piece = spec((8, half // 8, cols), lambda i, s: (0, 0, 0))
    return call(
        joint_kernel,
        (2,),
        [feature, feature, whole(gq), whole(gq), whole(gk), whole(gv)],
        [piece, piece],
        [shape((8, half // 8, cols), bf16)] * 2,
        (n_own, n_far, gq, gq_far, gk, gv),
        scalars,
        28,
    )


def back_qkv_kernel(s, gq_o, gq_f, gk, gv, wq, wk, wv, own, far):
    rows = own.shape[0]

    def part(gq, at):
        total = dot(gq[...], wq[...], NT)
        total += dot(gk[pl.ds(at, rows)], wk[...], NT)
        return total + dot(gv[pl.ds(at, rows)], wv[...], NT)

    far[...] = part(gq_f, rows).astype(bf16)
    own[...] = part(gq_o, 0)


def back_qkv(scalars, gq, gq_far, gk, gv, w):
    rows, half = gq.shape
    width = 2 * half

    def column(part):
        return spec((width, half), lambda i, s: (0, 2 * part + s[1]))

    full = spec((rows, width), lambda i, s: (0, 0))
    return call(
        back_qkv_kernel,
        (1,),
        [whole(gq), whole(gq), whole(gk), whole(gv), column(0), column(1), column(2)],
        [full, full],
        [shape((rows, width), f32), shape((rows, width), bf16)],
        (gq, gq_far, gk, gv, w, w, w),
        scalars,
        28,
    )


def last_kernel(s, own, far, resid, gain, grad2, out):
    xhat, scale = normalize(resid[...])
    grad = own[...] + far[...].astype(f32)
    out[...] = grad2[...] + norm_backward(grad, gain[...], xhat, scale)


def token_grad(scalars, own, far, resid, gain, grad2):
    args = (own, far, resid, gain, grad2)
    return call(
        last_kernel,
        (1,),
        [whole(a) for a in args],
        whole(own),
        shape(own.shape, f32),
        args,
        scalars,
        24,
    )


def row_sums(values):
    folded = sum(values[:, at : at + 128] for at in range(0, values.shape[1], 128))
    return lax.dot_general(
        jnp.ones((8, 128), f32),
        folded,
        (NT, ((), ())),
        precision=lax.Precision.HIGHEST,
        preferred_element_type=f32,
    )


def unpack_ff_kernel(at, last, s, own, other, w, gain_in, *refs):
    gain, down, up, *proj = refs[-4:] if last else refs[-3:]
    step = pl.program_id(0)

    def unpack(source, code):
        for block in range(8):
            to = block ^ (code & 7)
            down[pl.ds(pl.multiple_of(to * 32, 32), 32), :] = source[block, :32, :].astype(f32)
            row = pl.multiple_of(to * 48, 16)
            up[pl.ds(row, 32), :] = source[block, 32:64, :512].astype(f32)
            up[pl.ds(row + 32, 16), :256] = source[block, 32:48, 512:].astype(f32)
            up[pl.ds(row + 32, 16), 256:] = source[block, 48:64, 512:].astype(f32)
            if last:
                wide = source.shape[2] // 2
                proj[0][pl.ds(row, 16), :] = source[block, 64:80, :wide].astype(f32)
                proj[0][pl.ds(row + 16, 16), :] = source[block, 64:80, wide:].astype(f32)
                proj[0][pl.ds(row + 32, 16), :] = source[block, 80:, :wide].astype(f32)

    @pl.when(step == 0)
    def _():
        unpack(own, s[at])

    @pl.when(step == 1)
    def _():
        unpack(other, s[at + 1])

    gain[0, 0] = gain_in[0, 0] + row_sums(up[...] * w[...].astype(f32))


def unpack_ff(scalars, chunk, far, own, other, w, so_far):
    width, hidden = w.shape
    at = 2 + 2 * chunk
    last = own.shape[1] > 64

    def side(i, s):
        return (s[at + i] // 8) ^ far

    def half(i, s):
        return 2 * chunk + (s[0] ^ i)

    any_spec = pl.BlockSpec(memory_space=pl.ANY)
    column = spec((width // 2, 512), lambda i, s: (side(i, s), half(i, s)))
    gain = spec((1, 1, 8, width // 2), lambda i, s: (i, side(i, s), 0, 0))
    out_specs = [gain, spec((256, width), lambda i, s: (2 * half(i, s) + side(i, s), 0)), column]
    out_shape = [shape((2, 2, 8, width // 2), f32), shape((hidden, width), f32), shape((width, hidden), f32)]
    if last:
        out_specs.append(spec((width // 2, width // 2), lambda i, s: (s[0] ^ i, side(i, s))))
        out_shape.append(shape((width, width), f32))
    in_specs = [whole(own), whole(other), column]
    in_specs += [gain, any_spec, any_spec, any_spec][: len(so_far)]
    return call(
        functools.partial(unpack_ff_kernel, at, last),
        (2,),
        in_specs,
        out_specs,
        out_shape,
        (own, other, w) + tuple(so_far),
        scalars,
        28,
        aliases={4 + i: i for i in range(len(so_far))},
    )


def unpack_qkv_kernel(s, own, other, w, *refs):
    joint, gain = refs[-2:]
    step = pl.program_id(0)
    mine = s[1]

    def unpack(source, code):
        half = source.shape[2] // 6

        def place_columns(first):
            for block in range(2):
                rows = pl.ds(pl.multiple_of((block ^ (code & 1)) * 48, 16), 48)
                for part in range(3):
                    for side in range(2):
                        column = 2 * half * part + half * (first ^ side)
                        value = source[block, :, (3 * side + part) * half : (3 * side + part + 1) * half]
                        joint[rows, column : column + half] = value.astype(f32)

        for first in range(2):
            pl.when(mine == first)(functools.partial(place_columns, first))

    @pl.when(step < 2)
    def _():
        unpack(own, s[8])

    @pl.when(step >= 2)
    def _():
        unpack(other, s[9])

    gain[0] = row_sums(joint[...] * w[...].astype(f32))


def unpack_qkv(scalars, far, own, other, w, so_far):
    width = w.shape[0]

    def row(i, s):
        code = s[8 + i // 2]
        return 4 * (s[0] ^ (i // 2)) + 2 * ((code // 4) ^ far) + ((i & 1) ^ ((code // 2) & 1))

    def blocks(mine):
        return spec((2,) + own.shape[1:], lambda i, s: (jnp.clip(i - 2 * mine, 0, 1), 0, 0))

    any_spec = pl.BlockSpec(memory_space=pl.ANY)
    rows = spec((width // 8, 3 * width), lambda i, s: (row(i, s), 0))
    return call(
        unpack_qkv_kernel,
        (4,),
        [blocks(0), blocks(1), rows] + [any_spec] * len(so_far),
        [rows, spec((1, 8, width // 8), lambda i, s: (row(i, s), 0, 0))],
        [shape((width, 3 * width), f32), shape((8, 8, width // 8), f32)],
        (own, other, w) + tuple(so_far),
        scalars,
        28,
        aliases={4 + i: i for i in range(len(so_far))},
    )


def fast(tokens, visible, ln1_gain, w_qkv, w_proj, ln2_gain, w_up, w_down, d_out):
    tok, cot = tokens[0], d_out[0]
    rows, width = tok.shape
    gain1, gain2 = ln1_gain[None], ln2_gain[None]
    scalars = [lax.axis_index("dp") & 1, lax.axis_index("blk")]
    for orders in FF_ORDERS + (QKV_ORDER,):
        scalars.extend(places(orders))
    scalars = jnp.stack([jnp.int32(v) for v in scalars])

    order = Order()
    run = order.run
    vis_far = swap(visible, "y")
    tok_far = swap(tok, "y")
    half = width // 2
    freqs = jnp.exp(jnp.arange(half, dtype=f32) * (-math.log(10000.0) / half))[None]
    pos = run(functools.partial(positions, scalars), visible, freqs)
    normed1, qkv, resid = run(functools.partial(ln_qkv, scalars, False), tok, pos, gain1, w_qkv)
    sums = run(functools.partial(attention, scalars), qkv, qkv)
    pos_far = run(functools.partial(positions, scalars), vis_far, freqs)
    normed1_far, kv_far = run(functools.partial(ln_qkv, scalars, True), tok_far, pos_far, gain1, w_qkv)
    attended = run(functools.partial(attention, scalars), qkv, kv_far, *sums)
    resid2, normed2, packed = run(
        functools.partial(project, scalars), attended, w_proj, resid, gain2
    )
    early = tuple(order.swap(array, "c") for array in (cot, packed))

    streams, blocks, values = {}, {}, {"early": early}
    ff, proj, joint = (jnp.zeros((2, 2, 8, width // 2), f32),), (), ()

    def feed_forward(first):
        if first == 0:
            send, keep, *values["sums"] = run(
                functools.partial(ff_chunks, scalars, 0, 1), normed2, cot, w_up, w_down
            )
            values["act", 0], values["e0"] = keep, order.swap(send, "c")
            return
        more = (*values["sums"], resid2, gain2, w_proj, w_proj)
        send1, keep1, send2, keep2, out, grad2, branch, g_own, g_other = run(
            functools.partial(ff_chunks, scalars, 1, 2), normed2, cot, w_up, w_down, *more
        )
        values["act", 1], values["e1"] = keep1, order.swap(send1, "c")
        values["act", 2], values["e2"] = keep2, order.swap(send2, "c")
        values["branch"], values["branch_other"] = branch, order.swap(branch, "c")
        values["g"] = order.swap(g_other, "y")
        values.update(out=out, grad2=grad2, own=g_own)

    def weight_grads(chunk):
        early = (*values["early"], packed)
        more = ()
        if chunk == 2:
            more = (attended, values["early"][1], values["branch"], values["branch_other"])
        keep, send = run(
            functools.partial(ff_grads, scalars, chunk),
            values["act", chunk], values["e%d" % chunk], cot, *early, *more,
        )
        streams[chunk] = total(order, keep, send, list(zip(*FF_ORDERS[chunk])))
        advance(chunk)

    def advance(chunk):
        pair = next(streams[chunk])
        if pair is not None:
            blocks.setdefault(chunk, []).append(pair)

    def wait(key):
        if key[0] in "nf" and key[1:].isdigit():
            chunk, far = int(key[1:]), int(key[0] == "f")
            own, other = blocks[chunk][far]
            blocks[chunk][far] = own, run(lambda value: value, other)
            return
        value = values[key]
        values[key] = run(lambda *v: v if isinstance(value, tuple) else v[0], *(value if isinstance(value, tuple) else (value,)))

    def own_queries():
        values["attn"] = run(functools.partial(attention_back, scalars), qkv, values["own"], qkv, kv_far)

    def far_queries():
        gq, *sums = values["attn"]
        values["q"] = run(functools.partial(far_query, scalars), normed1_far, w_qkv)
        back = run(functools.partial(attention_back, scalars), values["q"], values["g"], qkv, kv_far, *sums)
        values["attn"] = (gq, *back)

    def joint_weights():
        keep, send = run(functools.partial(joint_grads, scalars), normed1, normed1_far, *values["attn"])
        links = [("c", "c")] + list(zip(*QKV_ORDER))
        streams[3] = total(order, keep, send, links, lambda a, b: jnp.concatenate([a, b], -1))
        advance(3)

    def back_joint():
        own, far = run(functools.partial(back_qkv, scalars), *values["attn"], w_qkv)
        values["norm"], values["bf"] = own, order.swap(far, "y")

    def finish_tokens():
        args = (values["norm"], values["bf"], resid, gain1, values["grad2"])
        values["tokens"] = run(functools.partial(token_grad, scalars), *args)

    def unpack(chunk, far):
        nonlocal ff, proj, joint
        own, other = blocks[chunk][far]
        if chunk == 3:
            joint = run(lambda a, b, *f: unpack_qkv(scalars, far, a, b, w_qkv, f), own, other, *joint)
            return
        so_far = ff + proj if chunk == 2 else ff
        weight = w_hbm if (chunk, far) == final else w_up
        result = tuple(
            run(lambda a, b, *f: unpack_ff(scalars, chunk, far, a, b, weight, f), own, other, *so_far)
        )
        ff, proj = result[:3], result[3:] or proj

    w_hbm = pltpu.with_memory_space_constraint(w_up, pltpu.HBM)
    final = [step[1:] for step in PLAN if step[0] == "unpack" and step[1] != 3][-1]
    steps = {
        "ff": feed_forward,
        "dw": weight_grads,
        "go": advance,
        "wait": wait,
        "own": own_queries,
        "far": far_queries,
        "joint": joint_weights,
        "back": back_joint,
        "tokens": finish_tokens,
        "unpack": unpack,
    }
    for name, *args in PLAN:
        steps[name](*args)
    sums2, d_down, d_up = ff
    d_qkv, sums1 = joint
    out, d_tokens, d_proj = values["out"], values["tokens"], proj[0]
    d_gain1 = sums1[:, 0].reshape(-1) / ln1_gain
    d_gain2 = (sums2[0, :, 0] + sums2[1, :, 0]).reshape(-1) / ln2_gain
    return out[None], d_tokens[None], d_gain1, d_qkv, d_proj, d_gain2, d_up, d_down


def layer_norm(values, gain):
    center = values - jnp.mean(values, -1, keepdims=True)
    spread = jnp.mean(center * center, -1, keepdims=True)
    return center * lax.rsqrt(spread + epsilon) * gain


def outer_product(left, right):
    return lax.dot_general(
        left, right, (((0,), (0,)), ((), ())), preferred_element_type=jnp.float32
    )


def times_transposed(left, weight):
    return lax.dot_general(
        left, weight, (((1,), (1,)), ((), ())), preferred_element_type=jnp.float32
    )


def split_blocks(keys, values):
    count = keys.shape[0]
    size = math.gcd(count, 512)
    shape = (count // size, size, HEADS, HD)
    return (keys.reshape(shape), values.reshape(shape))


def general(tokens, visible, ln1_gain, w_qkv, w_proj, ln2_gain, w_up, w_down, d_out):
    rows = tokens.shape[1]
    width = tokens.shape[2]
    factor = HD ** (-0.5)
    resid = tokens[0].astype(jnp.float32) + position_table(visible[0], width)
    normed1, back_one = jax.vjp(layer_norm, resid, ln1_gain)
    normed1 = normed1.astype(jnp.bfloat16)
    qkv = jnp.dot(normed1, w_qkv, preferred_element_type=jnp.float32).astype(jnp.bfloat16)
    query = qkv[:, :width]
    keys = qkv[:, width : 2 * width]
    values = qkv[:, 2 * width :]
    query_heads = query.reshape(rows, HEADS, HD)
    initial = (
        jnp.full((HEADS, rows), -1e30, jnp.float32),
        jnp.zeros((HEADS, rows), jnp.float32),
        jnp.zeros((HEADS, rows, HD), jnp.float32),
    )
    key_blocks, value_blocks = split_blocks(
        lax.all_gather(keys, "blk", axis=0, tiled=True),
        lax.all_gather(values, "blk", axis=0, tiled=True),
    )

    def one_block(state, block):
        running, total, accum = state
        block_keys, block_values = block
        scores = (
            jnp.einsum("qhd,khd->hqk", query_heads, block_keys, preferred_element_type=jnp.float32)
            * factor
        )
        top = jnp.maximum(running, jnp.max(scores, -1))
        weights = jnp.exp(scores - top[..., None])
        shrink = jnp.exp(running - top)
        total = total * shrink + jnp.sum(weights, -1)
        accum = accum * shrink[..., None] + jnp.einsum(
            "hqk,khd->hqd",
            weights.astype(jnp.bfloat16),
            block_values,
            preferred_element_type=jnp.float32,
        )
        return ((top, total, accum), None)

    running, total, accum = lax.scan(one_block, initial, (key_blocks, value_blocks))[0]
    log_total = running + jnp.log(total)
    attended = (accum / total[..., None]).transpose(1, 0, 2).reshape(rows, width)
    attended_low = attended.astype(jnp.bfloat16)
    resid2 = resid + jnp.dot(attended_low, w_proj, preferred_element_type=jnp.float32)
    normed2, back_two = jax.vjp(layer_norm, resid2, ln2_gain)
    normed2 = normed2.astype(jnp.bfloat16)
    hidden = jnp.dot(normed2, w_up, preferred_element_type=jnp.float32)
    activated, back_gelu = jax.vjp(jax.nn.gelu, hidden)
    activated = activated.astype(jnp.bfloat16)
    result = resid2 + jnp.dot(activated, w_down, preferred_element_type=jnp.float32)
    cotangent = d_out[0]
    grad_down = outer_product(activated, cotangent)
    (grad_hidden,) = back_gelu(times_transposed(cotangent, w_down))
    grad_hidden = grad_hidden.astype(jnp.bfloat16)
    grad_up = outer_product(normed2, grad_hidden)
    grad_resid2, grad_gain2 = back_two(times_transposed(grad_hidden, w_up))
    grad_resid2 = grad_resid2 + cotangent.astype(jnp.float32)
    grad_branch = grad_resid2.astype(jnp.bfloat16)
    grad_proj = outer_product(attended_low, grad_branch)
    grad_attended = times_transposed(grad_branch, w_proj).astype(jnp.bfloat16)
    correction = (grad_attended.astype(jnp.float32) * attended).reshape(rows, HEADS, HD)
    correction = jnp.sum(correction, -1).T
    grad_heads = grad_attended.reshape(rows, HEADS, HD)
    all_keys, all_values = (
        lax.all_gather(keys, "blk", axis=0, tiled=True),
        lax.all_gather(values, "blk", axis=0, tiled=True),
    )
    full_rows = all_keys.shape[0]
    key_blocks, value_blocks = split_blocks(all_keys, all_values)

    def back_block(grad_query, block):
        block_keys, block_values = block
        scores = (
            jnp.einsum("qhd,khd->hqk", query_heads, block_keys, preferred_element_type=jnp.float32)
            * factor
        )
        probs = jnp.exp(scores - log_total[..., None])
        grad_value = jnp.einsum(
            "hqk,qhd->khd",
            probs.astype(jnp.bfloat16),
            grad_heads,
            preferred_element_type=jnp.float32,
        )
        grad_probs = jnp.einsum(
            "qhd,khd->hqk", grad_heads, block_values, preferred_element_type=jnp.float32
        )
        grad_scores = (probs * (grad_probs - correction[..., None])).astype(jnp.bfloat16)
        grad_query = grad_query + jnp.einsum(
            "hqk,khd->qhd", grad_scores, block_keys, preferred_element_type=jnp.float32
        )
        grad_key = (
            jnp.einsum("hqk,qhd->khd", grad_scores, query_heads, preferred_element_type=jnp.float32)
            * factor
        )
        return (grad_query, (grad_key, grad_value))

    grad_query, (key_parts, value_parts) = lax.scan(
        back_block, jnp.zeros((rows, HEADS, HD), jnp.float32), (key_blocks, value_blocks)
    )
    grad_query = (grad_query * factor).reshape(rows, width)
    grad_keys, grad_values = (
        lax.psum_scatter(
            key_parts.reshape(full_rows, width).astype(jnp.bfloat16),
            "blk",
            scatter_dimension=0,
            tiled=True,
        ).astype(jnp.float32),
        lax.psum_scatter(
            value_parts.reshape(full_rows, width).astype(jnp.bfloat16),
            "blk",
            scatter_dimension=0,
            tiled=True,
        ).astype(jnp.float32),
    )
    grad_qkv = jnp.concatenate([grad_query, grad_keys, grad_values], 1).astype(jnp.bfloat16)
    grad_joint = outer_product(normed1, grad_qkv)
    grad_resid, grad_gain1 = back_one(times_transposed(grad_qkv, w_qkv))
    input_grad = grad_resid2 + grad_resid
    flats = (
        grad_joint.reshape(-1),
        grad_proj.reshape(-1),
        grad_up.reshape(-1),
        grad_down.reshape(-1),
    )
    shares = (
        lax.psum_scatter(flats[0], ("dp", "blk"), scatter_dimension=0, tiled=True),
        lax.psum_scatter(flats[1], ("dp", "blk"), scatter_dimension=0, tiled=True),
        lax.psum_scatter(flats[2], ("dp", "blk"), scatter_dimension=0, tiled=True),
        lax.psum_scatter(flats[3], ("dp", "blk"), scatter_dimension=0, tiled=True),
    )
    summed = (
        lax.all_gather(shares[0].astype(jnp.bfloat16), ("dp", "blk"), axis=0, tiled=True).astype(
            jnp.float32
        ),
        lax.all_gather(shares[1].astype(jnp.bfloat16), ("dp", "blk"), axis=0, tiled=True).astype(
            jnp.float32
        ),
        lax.all_gather(shares[2].astype(jnp.bfloat16), ("dp", "blk"), axis=0, tiled=True).astype(
            jnp.float32
        ),
        lax.all_gather(shares[3].astype(jnp.bfloat16), ("dp", "blk"), axis=0, tiled=True).astype(
            jnp.float32
        ),
    )
    gain_one, gain_two = lax.psum((grad_gain1, grad_gain2), ("dp", "blk"))
    return (
        result.astype(jnp.bfloat16)[None],
        input_grad[None],
        gain_one,
        summed[0].reshape(w_qkv.shape),
        summed[1].reshape(w_proj.shape),
        gain_two,
        summed[2].reshape(w_up.shape),
        summed[3].reshape(w_down.shape),
    )


def solution(mesh):
    split = mesh.shape["dp"] == 16 and mesh.shape["blk"] == 2

    def local(tokens, *others):
        fits = split and 2 * tokens.shape[1] == tokens.shape[2]
        return (fast if fits else general)(tokens, *others)

    return jax.shard_map(
        local,
        mesh=mesh,
        in_specs=(
            P("dp", "blk", None),
            P("dp", "blk"),
            P(),
            P(),
            P(),
            P(),
            P(),
            P(),
            P("dp", "blk", None),
        ),
        out_specs=(P("dp", "blk", None), P("dp", "blk", None), P(), P(), P(), P(), P(), P()),
        check_vma=False,
    )
```

profile of v0, /device:TPU:0, one launch (start us, length us, event | category | flops | bytes accessed | tf_op | source)
XLA Modules:
  0.0 192.6 jit_solution(16330167877022629377)
XLA Ops:
  0.6 3.0 %collective-permute-start = (bf16[384,768]{1,0:T(8,128)(2,1)}, bf16[384,768]{1,0:T(8,128)(2,1)}, u32[]{:S(2)}, u32[]{:S(2)}) collective-permute-start(bf16[384,768]{1,0:T(8,128)(2,1)} %bitcast.22), channel_id=1, source_target_pairs={{0,1},{1,0},{2,3},{3,2},{4,5},{5,4},{6,7},{7,6},{8,9},{9,8},{10,11... | collective-permute-start | bytes 1769480 | tf_op jit(solution)/shard_map/ppermute | solution.py:111
  6.1 2.0 %copy-done = bf16[768,2304]{1,0:T(8,128)(2,1)S(1)} copy-done((bf16[768,2304]{1,0:T(8,128)(2,1)S(1)}, bf16[768,2304]{1,0:T(8,128)(2,1)}, u32[]{:S(2)}) %copy-start) | copy-done | bytes 3538968
  8.1 3.2 %shard_map.153 = (bf16[384,768]{1,0:T(8,128)(2,1)S(1)}, bf16[384,2304]{1,0:T(8,128)(2,1)S(1)}, f32[384,768]{1,0:T(8,128)S(1)}) custom-call(s32[10]{0:T(128)S(1)} %stack.37.s, bf16[384,768]{1,0:T(8,128)(2,1)S(1)} %bitcast.23, f32[384,768]{1,0:T(8,128)S(1)} %shard_map.152.pos, f32[1,768]{1,0:T(1,128)S(1)} %broadcast_in_dim.16.gain, bf16[768,2304]{1,0:T(8,128)(2,1)S(1)} %copy-done), custom_call_target="tpu_custom_call" | custom-call | flops 1 | bytes 1 | tf_op jit(solution)/shard_map/pallas_call | solution.py:54
  11.4 4.4 %shard_map.154 = (f32[6,128,384]{2,1,0:T(8,128)S(1)}, f32[6,8,768]{2,1,0:T(8,128)S(1)}) custom-call(s32[10]{0:T(128)S(1)} %stack.37.s, bf16[384,2304]{1,0:T(8,128)(2,1)S(1)} %get-tuple-element.426.q.k.v.k_o.v_o, bf16[384,2304]{1,0:T(8,128)(2,1)S(1)} %get-tuple-element.426.q.k.v.k_o.v_o, bf16[384,2304]{1,0:T(8,128)(2,1)S(1)} %get-tuple-element.426.q.k.v.k_o.v_o), custom_call_target="tpu_custom_call" | custom-call | flops 1 | bytes 1 | tf_op jit(solution)/shard_map/pallas_call | solution.py:54
  18.9 3.5 %shard_map.156 = (bf16[384,768]{1,0:T(8,128)(2,1)S(1)}, bf16[384,1536]{1,0:T(8,128)(2,1)S(1)}) custom-call(s32[10]{0:T(128)S(1)} %stack.37.s, bf16[384,768]{1,0:T(8,128)(2,1)} %collective-permute-done.tok, f32[384,768]{1,0:T(8,128)S(1)} %shard_map.155.pos, f32[1,768]{1,0:T(1,128)S(1)} %broadcast_in_dim.16.gain, bf16[768,2304]{1,0:T(8,128)(2,1)S(1)} %copy-done.1), custom_call_target="tpu_custom_call" | custom-call | flops 1 | bytes 1 | tf_op jit(solution)/shard_map/pallas_call | solution.py:54
  22.4 4.6 %shard_map.157.att.att_half.refs_0_ = bf16[384,768]{1,0:T(8,128)(2,1)S(1)} custom-call(s32[10]{0:T(128)S(1)} %stack.37.s, bf16[384,2304]{1,0:T(8,128)(2,1)S(1)} %get-tuple-element.426.q.k.v.k_o.v_o, bf16[384,1536]{1,0:T(8,128)(2,1)S(1)} %get-tuple-element.427.k.v.k_f.v_f, bf16[384,1536]{1,0:T(8,128)(2,1)S(1)} %get-tuple-element.427.k.v.k_f.v_f, ...), custom_call_target="tpu_custom_call" | custom-call | flops 1 | bytes 1 | tf_op jit(solution)/shard_map/pallas_call | solution.py:54
  27.1 1.6 shard_map.158
  29.4 4.5 %shard_map.159 = (bf16[2,384,512]{2,1,0:T(8,128)(2,1)S(1)}, bf16[2,384,512]{2,1,0:T(8,128)(2,1)S(1)}, f32[384,768]{1,0:T(8,128)S(1)}, f32[384,768]{1,0:T(8,128)S(1)}) custom-call(s32[10]{0:T(128)S(1)} %stack.37.s, bf16[384,768]{1,0:T(8,128)(2,1)S(1)} %get-tuple-element.354.normed, bf16[384,768]{1,0:T(8,128)(2,1)S(1)} %bitcast.17, ...), custom_call_target="tpu_custom_call" | custom-call | flops 1 | bytes 1 | tf_op jit(solution)/shard_map/pallas_call | solution.py:54
  34.1 10.9 %shard_map.160 = (bf16[2,384,512]{2,1,0:T(8,128)(2,1)S(1)}, bf16[2,384,512]{2,1,0:T(8,128)(2,1)S(1)}, bf16[2,384,512]{2,1,0:T(8,128)(2,1)S(1)}, bf16[2,384,512]{...) custom-call(s32[10]{0:T(128)S(1)} %stack.37.s, ...), custom_call_target="tpu_custom_call" | custom-call | flops 1 | bytes 1 | tf_op jit(solution)/shard_map/pallas_call | solution.py:54
  45.5 1.7 collective-permute-start.9
  47.4 2.7 %shard_map.161 = (bf16[8,64,768]{2,1,0:T(8,128)(2,1)S(1)}, bf16[8,64,768]{2,1,0:T(8,128)(2,1)S(1)}) custom-call(s32[10]{0:T(128)S(1)} %stack.37.s, bf16[2,384,512]{2,1,0:T(8,128)(2,1)S(1)} %get-tuple-element.371.act.grad, bf16[2,384,512]{2,1,0:T(8,128)(2,1)S(1)} %collective-permute-done.4.act_o.grad_o, bf16[2,384,512]{2,1,0:T(8,128)(2,1)S(1)} %get-tuple-element.371.act.grad, ...), custom_call_target="tpu_custom_call" | custom-call | flops 1 | bytes 1 | tf_op jit(solution)/shard_map/pallas_call | solution.py:54
  50.1 1.6 collective-permute-start.5
  51.6 7.9 %shard_map.162 = (bf16[384,384]{1,0:T(8,128)(2,1)S(1)}, f32[768,384]{1,0:T(8,128)S(1)}, f32[768,384]{1,0:T(8,128)S(1)}) custom-call(s32[10]{0:T(128)S(1)} %stack.37.s, bf16[384,2304]{1,0:T(8,128)(2,1)S(1)} %get-tuple-element.426.q.k.v.k_o.v_o, bf16[384,384]{1,0:T(8,128)(2,1)S(1)} %get-tuple-element.379.g, ...), custom_call_target="tpu_custom_call" | custom-call | flops 1 | bytes 1 | tf_op jit(solution)/shard_map/pallas_call | solution.py:54
  59.6 3.5 %shard_map.163 = (bf16[8,96,768]{2,1,0:T(8,128)(2,1)S(1)}, bf16[8,96,768]{2,1,0:T(8,128)(2,1)S(1)}) custom-call(s32[10]{0:T(128)S(1)} %stack.37.s, bf16[2,384,512]{2,1,0:T(8,128)(2,1)S(1)} %get-tuple-element.397.act.grad, bf16[2,384,512]{2,1,0:T(8,128)(2,1)S(1)} %collective-permute-done.7.act_o.grad_o, bf16[2,384,512]{2,1,0:T(8,128)(2,1)S(1)} %get-tuple-element.397.act.grad, ...), custom_call_target="tpu_custom_call" | custom-call | flops 1 | bytes 1 | tf_op jit(solution)/shard_map/pallas_call | solution.py:54
  63.7 2.5 %shard_map.164 = (bf16[8,64,768]{2,1,0:T(8,128)(2,1)S(1)}, bf16[8,64,768]{2,1,0:T(8,128)(2,1)S(1)}) custom-call(s32[10]{0:T(128)S(1)} %stack.37.s, bf16[2,384,512]{2,1,0:T(8,128)(2,1)S(1)} %get-tuple-element.409.act.grad, bf16[2,384,512]{2,1,0:T(8,128)(2,1)S(1)} %collective-permute-done.6.act_o.grad_o, bf16[2,384,512]{2,1,0:T(8,128)(2,1)S(1)} %get-tuple-element.409.act.grad, ...), custom_call_target="tpu_custom_call" | custom-call | flops 1 | bytes 1 | tf_op jit(solution)/shard_map/pallas_call | solution.py:54
  66.2 1.6 collective-permute-start.16
  69.1 1.6 collective-permute-start.12
  70.7 8.4 %shard_map.166 = (bf16[384,384]{1,0:T(8,128)(2,1)S(1)}, bf16[768,384]{1,0:T(8,128)(2,1)S(1)}, bf16[768,384]{1,0:T(8,128)(2,1)S(1)}) custom-call(s32[10]{0:T(128)S(1)} %stack.37.s, bf16[384,384]{1,0:T(8,128)(2,1)S(1)} %shard_map.165.q, bf16[384,384]{1,0:T(8,128)(2,1)S(1)} %collective-permute-done.9.g, bf16[384,2304]{1,0:T(8,128)(2,1)S(1)} %get-tuple-element.426.q.k.v.k_o.v_o, ...), custom_call_target="tpu_custom_call" | custom-call | flops 1 | bytes 1 | tf_op jit(solution)/shard_map/pallas_call | solution.py:54
  79.5 1.6 collective-permute-start.11
  81.3 3.4 %shard_map.167 = (bf16[8,48,1152]{2,1,0:T(8,128)(2,1)S(1)}, bf16[8,48,1152]{2,1,0:T(8,128)(2,1)S(1)}) custom-call(s32[10]{0:T(128)S(1)} %stack.37.s, bf16[384,768]{1,0:T(8,128)(2,1)S(1)} %get-tuple-element.441.n_own, bf16[384,768]{1,0:T(8,128)(2,1)S(1)} %copy-done.9, bf16[384,384]{1,0:T(8,128)(2,1)S(1)} %get-tuple-element.474.gq_o, ...), custom_call_target="tpu_custom_call" | custom-call | flops 1 | bytes 1 | tf_op jit(solution)/shard_map/pallas_call | solution.py:54
  84.7 1.7 collective-permute-done.12
  86.4 1.9 collective-permute-start.15
  89.8 2.3 %collective-permute-done.15 = bf16[2,64,768]{2,1,0:T(8,128)(2,1)S(1)} collective-permute-done((bf16[2,64,768]{2,1,0:T(8,128)(2,1)S(1)}, bf16[2,64,768]{2,1,0:T(8,128)(2,1)S(1)}, u32[]{:S(2)}, u32[]{:S(2)}) %collective-permute-start.15) | collective-permute-done | bytes 196640 | tf_op jit(solution)/shard_map/ppermute | solution.py:111
  93.0 2.7 %collective-permute-start.18 = (bf16[2,64,768]{2,1,0:T(8,128)(2,1)S(1)}, bf16[2,64,768]{2,1,0:T(8,128)(2,1)S(1)}, u32[]{:S(2)}, u32[]{:S(2)}) collective-permute-start(bf16[2,64,768]{2,1,0:T(8,128)(2,1)S(1)} %add_convert_fusion.21), channel_id=1, source_target_pairs={{0,16},{1,17},{2,18},{3,19},{4,20},{5,21},{6,22},{7,23},{8,24},{9,... | collective-permute-start | bytes 589832 | tf_op jit(solution)/shard_map/ppermute | solution.py:111
  99.0 2.6 %shard_map.168 = (f32[384,768]{1,0:T(8,128)S(1)}, bf16[384,768]{1,0:T(8,128)(2,1)S(1)}) custom-call(s32[10]{0:T(128)S(1)} %stack.37.s, bf16[384,384]{1,0:T(8,128)(2,1)S(1)} %get-tuple-element.474.gq_o, bf16[384,384]{1,0:T(8,128)(2,1)S(1)} %get-tuple-element.475.gq_f, bf16[768,384]{1,0:T(8,128)(2,1)S(1)} %get-tuple-element.476.gk, ...), custom_call_target="tpu_custom_call" | custom-call | flops 1 | bytes 1 | tf_op jit(solution)/shard_map/pallas_call | solution.py:54
  102.0 2.5 %collective-permute-start.22 = (bf16[2,96,768]{2,1,0:T(8,128)(2,1)S(1)}, bf16[2,96,768]{2,1,0:T(8,128)(2,1)S(1)}, u32[]{:S(2)}, u32[]{:S(2)}) collective-permute-start(bf16[2,96,768]{2,1,0:T(8,128)(2,1)S(1)} %add_convert_fusion.9), channel_id=1, source_target_pairs={{0,16},{1,17},{2,18},{3,19},{4,20},{5,21},{6,22},{7,23},{8,24},{9,... | collective-permute-start | bytes 884744 | tf_op jit(solution)/shard_map/ppermute | solution.py:111
  104.8 1.8 collective-permute-start.21
  108.0 8.4 %collective-permute-done.17.far = bf16[384,768]{1,0:T(8,128)(2,1)S(1)} collective-permute-done((bf16[384,768]{1,0:T(8,128)(2,1)S(1)}, bf16[384,768]{1,0:T(8,128)(2,1)S(1)}, u32[]{:S(2)}, u32[]{:S(2)}) %collective-permute-start.17) | collective-permute-done | bytes 589856 | tf_op jit(solution)/shard_map/ppermute | solution.py:111
  116.4 7.3 %collective-permute-done.22 = bf16[2,96,768]{2,1,0:T(8,128)(2,1)S(1)} collective-permute-done((bf16[2,96,768]{2,1,0:T(8,128)(2,1)S(1)}, bf16[2,96,768]{2,1,0:T(8,128)(2,1)S(1)}, u32[]{:S(2)}, u32[]{:S(2)}) %collective-permute-start.22) | collective-permute-done | bytes 294944 | tf_op jit(solution)/shard_map/ppermute | solution.py:111
  125.7 6.8 %collective-permute-done.27 = bf16[2,96,768]{2,1,0:T(8,128)(2,1)S(1)} collective-permute-done((bf16[2,96,768]{2,1,0:T(8,128)(2,1)S(1)}, bf16[2,96,768]{2,1,0:T(8,128)(2,1)S(1)}, u32[]{:S(2)}, u32[]{:S(2)}) %collective-permute-start.27) | collective-permute-done | bytes 294944 | tf_op jit(solution)/shard_map/ppermute | solution.py:111
  132.7 2.9 %collective-permute-start.30 = (bf16[2,64,768]{2,1,0:T(8,128)(2,1)S(1)}, bf16[2,64,768]{2,1,0:T(8,128)(2,1)S(1)}, u32[]{:S(2)}, u32[]{:S(2)}) collective-permute-start(bf16[2,64,768]{2,1,0:T(8,128)(2,1)S(1)} %add_convert_fusion.17), channel_id=1, source_target_pairs={{0,16},{1,17},{2,10},{3,11},{4,20},{5,21},{6,14},{7,15},{8,24},{9,... | collective-permute-start | bytes 589832 | tf_op jit(solution)/shard_map/ppermute | solution.py:111
  137.5 6.6 %collective-permute-done.32 = bf16[2,48,1152]{2,1,0:T(8,128)(2,1)S(1)} collective-permute-done((bf16[2,48,1152]{2,1,0:T(8,128)(2,1)S(1)}, bf16[2,48,1152]{2,1,0:T(8,128)(2,1)S(1)}, u32[]{:S(2)}, u32[]{:S(2)}) %collective-permute-start.32) | collective-permute-done | bytes 221216 | tf_op jit(solution)/shard_map/ppermute | solution.py:111
  144.2 2.4 %collective-permute-done.31 = bf16[4,96,768]{2,1,0:T(8,128)(2,1)S(1)} collective-permute-done((bf16[4,96,768]{2,1,0:T(8,128)(2,1)S(1)}, bf16[4,96,768]{2,1,0:T(8,128)(2,1)S(1)}, u32[]{:S(2)}, u32[]{:S(2)}) %collective-permute-start.31) | collective-permute-done | bytes 589856 | tf_op jit(solution)/shard_map/ppermute | solution.py:111
  146.8 1.7 collective-permute-start.39
  149.1 1.8 collective-permute-done.28.own
  151.0 2.6 %shard_map.169 = (f32[2,2,8,384]{3,2,1,0:T(8,128)S(1)}, f32[3072,768]{1,0:T(8,128)}, f32[768,3072]{1,0:T(8,128)}) custom-call(s32[10]{0:T(128)S(1)} %stack.37.s, bf16[8,64,768]{2,1,0:T(8,128)(2,1)S(1)} %constant_dynamic-update-slice_fusion.4.own, bf16[8,64,768]{2,1,0:T(8,128)(2,1)S(1)} %collective-permute-done.29.other, ...), custom_call_target="tpu_custom_call", output_to_operand_aliasing={{0}: (4, {})} | custom-call | flops 1 | bytes 1 | tf_op jit(solution)/shard_map/pallas_call | solution.py:54
  153.6 3.5 %collective-permute-done.35 = bf16[2,48,2304]{2,1,0:T(8,128)(2,1)S(1)} collective-permute-done((bf16[2,48,2304]{2,1,0:T(8,128)(2,1)S(1)}, bf16[2,48,2304]{2,1,0:T(8,128)(2,1)S(1)}, u32[]{:S(2)}, u32[]{:S(2)}) %collective-permute-start.35) | collective-permute-done | bytes 442400 | tf_op jit(solution)/shard_map/ppermute | solution.py:111
  157.2 2.7 %collective-permute-start.36 = (bf16[4,48,2304]{2,1,0:T(8,128)(2,1)S(1)}, bf16[4,48,2304]{2,1,0:T(8,128)(2,1)S(1)}, u32[]{:S(2)}, u32[]{:S(2)}) collective-permute-start(bf16[4,48,2304]{2,1,0:T(8,128)(2,1)S(1)} %constant_dynamic-update-slice_fusion.10.own), channel_id=1, source_target_pairs={{0,4},{1,5},{2,10},{3,11},{4,0},{5,1},{6,14},{7,15},{8,12},{9,13},... | collective-permute-start | bytes 2654216 | tf_op jit(solution)/shard_map/ppermute | solution.py:111
  160.0 1.6 collective-permute-start.37
  161.5 2.4 %shard_map.170 = f32[384,768]{1,0:T(8,128)} custom-call(s32[10]{0:T(128)S(1)} %stack.37.s, f32[384,768]{1,0:T(8,128)S(1)} %get-tuple-element.542.own, bf16[384,768]{1,0:T(8,128)(2,1)S(1)} %collective-permute-done.17.far, f32[384,768]{1,0:T(8,128)S(1)} %copy-done.7, f32[1,768]{1,0:T(1,128)S(1)} %broadcast_in_dim.16.gain, f32[384,768]{1,0:T(8,128)S(1)} %copy-done.11), custom_call_target="tpu_custom_call" | custom-call | flops 1 | bytes 1 | tf_op jit(solution)/shard_map/pallas_call | solution.py:54
  163.9 2.6 %shard_map.171 = (f32[2,2,8,384]{3,2,1,0:T(8,128)S(1)}, f32[3072,768]{1,0:T(8,128)}, f32[768,3072]{1,0:T(8,128)}) custom-call(s32[10]{0:T(128)S(1)} %stack.37.s, bf16[8,64,768]{2,1,0:T(8,128)(2,1)S(1)} %collective-permute-done.28.own, ...), custom_call_target="tpu_custom_call", output_to_operand_aliasing={{0}: (4, {}), {1}: (5, {}), {2}: (6, {})} | custom-call | flops 1 | bytes 1 | tf_op jit(solution)/shard_map/pallas_call | solution.py:54
  167.5 3.1 %shard_map.172 = (f32[2,2,8,384]{3,2,1,0:T(8,128)S(1)}, f32[3072,768]{1,0:T(8,128)}, f32[768,3072]{1,0:T(8,128)}, f32[768,768]{1,0:T(8,128)}) custom-call(s32[10]{0:T(128)S(1)} %stack.37.s, bf16[8,96,768]{2,1,0:T(8,128)(2,1)S(1)} %constant_dynamic-update-slice_fusion.8.own, ...), custom_call_target="tpu_custom_call", output_to_operand_aliasing={{0}: (4, {}), {1}: (5, {}), {2}: (6, {})} | custom-call | flops 1 | bytes 1 | tf_op jit(solution)/shard_map/pallas_call | solution.py:54
  170.6 2.4 %collective-permute-done.37 = bf16[4,64,768]{2,1,0:T(8,128)(2,1)S(1)} collective-permute-done((bf16[4,64,768]{2,1,0:T(8,128)(2,1)S(1)}, bf16[4,64,768]{2,1,0:T(8,128)(2,1)S(1)}, u32[]{:S(2)}, u32[]{:S(2)}) %collective-permute-start.37) | collective-permute-done | bytes 393248 | tf_op jit(solution)/shard_map/ppermute | solution.py:111
  174.7 3.1 %shard_map.173 = (f32[2,2,8,384]{3,2,1,0:T(8,128)S(1)}, f32[3072,768]{1,0:T(8,128)}, f32[768,3072]{1,0:T(8,128)}, f32[768,768]{1,0:T(8,128)}) custom-call(s32[10]{0:T(128)S(1)} %stack.37.s, bf16[8,96,768]{2,1,0:T(8,128)(2,1)S(1)} %collective-permute-done.39.own, ...), custom_call_target="tpu_custom_call", output_to_operand_aliasing={{0}: (4, {}), {1}: (5, {}), {2}: (6, {}), {3}: (7, {})} | custom-call | flops 1 | bytes 1 | tf_op jit(solution)/shard_map/pallas_call | solution.py:54
  177.8 3.2 %shard_map.174 = (f32[768,2304]{1,0:T(8,128)}, f32[8,8,96]{2,1,0:T(8,128)S(1)}) custom-call(s32[10]{0:T(128)S(1)} %stack.37.s, bf16[4,48,2304]{2,1,0:T(8,128)(2,1)S(1)} %constant_dynamic-update-slice_fusion.10.own, bf16[4,48,2304]{2,1,0:T(8,128)(2,1)S(1)} %collective-permute-done.41.other, bf16[768,2304]{1,0:T(8,128)(2,1)S(1)} %copy-done.1), custom_call_target="tpu_custom_call" | custom-call | flops 1 | bytes 1 | tf_op jit(solution)/shard_map/pallas_call | solution.py:54
  181.0 3.2 %shard_map.175 = (f32[768,2304]{1,0:T(8,128)}, f32[8,8,96]{2,1,0:T(8,128)S(1)}) custom-call(s32[10]{0:T(128)S(1)} %stack.37.s, bf16[4,48,2304]{2,1,0:T(8,128)(2,1)S(1)} %collective-permute-done.36.own, bf16[4,48,2304]{2,1,0:T(8,128)(2,1)S(1)} %collective-permute-done.40.other, ...), custom_call_target="tpu_custom_call", output_to_operand_aliasing={{0}: (4, {}), {1}: (5, {})} | custom-call | flops 1 | bytes 1 | tf_op jit(solution)/shard_map/pallas_call | solution.py:54
  185.2 2.6 %shard_map.176 = (f32[2,2,8,384]{3,2,1,0:T(8,128)S(1)}, f32[3072,768]{1,0:T(8,128)}, f32[768,3072]{1,0:T(8,128)}) custom-call(s32[10]{0:T(128)S(1)} %stack.37.s, bf16[8,64,768]{2,1,0:T(8,128)(2,1)S(1)} %constant_dynamic-update-slice_fusion.14.own, ...), custom_call_target="tpu_custom_call", output_to_operand_aliasing={{0}: (4, {}), {1}: (5, {}), {2}: (6, {})} | custom-call | flops 1 | bytes 1 | tf_op jit(solution)/shard_map/pallas_call | solution.py:54
  188.5 3.5 %shard_map.177 = (f32[2,2,8,384]{3,2,1,0:T(8,128)S(1)}, f32[3072,768]{1,0:T(8,128)}, f32[768,3072]{1,0:T(8,128)}) custom-call(s32[10]{0:T(128)S(1)} %stack.37.s, bf16[8,64,768]{2,1,0:T(8,128)(2,1)S(1)} %collective-permute-done.43.own, ...), custom_call_target="tpu_custom_call", output_to_operand_aliasing={{0}: (4, {}), {1}: (5, {}), {2}: (6, {})} | custom-call | flops 1 | bytes 1 | tf_op jit(solution)/shard_map/pallas_call | solution.py:54
  (163 shorter events, 27.0 us)
Async XLA Ops:
  0.6 18.2 %collective-permute-start = (bf16[384,768]{1,0:T(8,128)(2,1)}, bf16[384,768]{1,0:T(8,128)(2,1)}, u32[]{:S(2)}, u32[]{:S(2)}) collective-permute-start(bf16[384,768]{1,0:T(8,128)(2,1)} %bitcast.22), channel_id=1, source_target_pairs={{0,1},{1,0},{2,3},{3,2},{4,5},{5,4},{6,7},{7,6},{8,9},{9,8},{10,11... | collective-permute-start | bytes 1769480 | tf_op jit(solution)/shard_map/ppermute | solution.py:111
  3.7 13.7 %collective-permute-start.1 = (s32[1,384]{1,0:T(1,128)}, s32[1,384]{1,0:T(1,128)S(1)}, u32[]{:S(2)}, u32[]{:S(2)}) collective-permute-start(s32[1,384]{1,0:T(1,128)} %visible.1), channel_id=1, source_target_pairs={{0,1},{1,0},{2,3},{3,2},{4,5},{5,4},{6,7},{7,6},{8,9},{9,8},{10,11... | collective-permute-start | bytes 4616 | tf_op jit(solution)/shard_map/ppermute | solution.py:111
  11.4 18.0 %slice-start.2 = ((s8[4718592]{0:T(1024)(128)(4,1)}), s8[4194304]{0:T(1024)(128)(4,1)S(1)}, s32[]{:S(2)}) async-start(s8[4718592]{0:T(1024)(128)(4,1)} %bitcast.14), calls=%async_computation.2 | async-start | bytes 8388608
  28.7 18.6 %copy-start.4 = (bf16[1152,384]{1,0:T(8,128)(2,1)}, bf16[1152,384]{1,0:T(8,128)(2,1)S(1)}, u32[]{:S(2)}) copy-start(bf16[1152,384]{1,0:T(8,128)(2,1)S(1)} %get-tuple-element.413.nt) | copy-start | bytes 2654212
  28.8 5.3 %collective-permute-start.3 = (bf16[1152,384]{1,0:T(8,128)(2,1)S(1)}, bf16[1152,384]{1,0:T(8,128)(2,1)S(1)}, u32[]{:S(2)}, u32[]{:S(2)}) collective-permute-start(bf16[1152,384]{1,0:T(8,128)(2,1)S(1)} %get-tuple-element.413.nt), channel_id=1, source_target_pairs={{0,2},{1,3},{2,0},{3,1},{4,6},{5,7},{6,4},{7,5},{8,10},{9,11},{10,... | collective-permute-start | bytes 2654216 | tf_op jit(solution)/shard_map/ppermute | solution.py:111
  28.9 5.2 %collective-permute-start.2 = (bf16[384,768]{1,0:T(8,128)(2,1)S(1)}, bf16[384,768]{1,0:T(8,128)(2,1)S(1)}, u32[]{:S(2)}, u32[]{:S(2)}) collective-permute-start(bf16[384,768]{1,0:T(8,128)(2,1)S(1)} %bitcast.16), channel_id=1, source_target_pairs={{0,2},{1,3},{2,0},{3,1},{4,6},{5,7},{6,4},{7,5},{8,10},{9,11},{10,... | collective-permute-start | bytes 1769480 | tf_op jit(solution)/shard_map/ppermute | solution.py:111
  33.9 13.4 %collective-permute-start.4 = (bf16[2,384,512]{2,1,0:T(8,128)(2,1)S(1)}, bf16[2,384,512]{2,1,0:T(8,128)(2,1)S(1)}, u32[]{:S(2)}, u32[]{:S(2)}) collective-permute-start(bf16[2,384,512]{2,1,0:T(8,128)(2,1)S(1)} %get-tuple-element.367), channel_id=1, source_target_pairs={{0,2},{1,3},{2,0},{3,1},{4,6},{5,7},{6,4},{7,5},{8,10},{9,11},{10,... | collective-permute-start | bytes 2359304 | tf_op jit(solution)/shard_map/ppermute | solution.py:111
  45.0 14.6 %collective-permute-start.7 = (bf16[2,384,512]{2,1,0:T(8,128)(2,1)S(1)}, bf16[2,384,512]{2,1,0:T(8,128)(2,1)S(1)}, u32[]{:S(2)}, u32[]{:S(2)}) collective-permute-start(bf16[2,384,512]{2,1,0:T(8,128)(2,1)S(1)} %get-tuple-element.389), channel_id=1, source_target_pairs={{0,2},{1,3},{2,0},{3,1},{4,6},{5,7},{6,4},{7,5},{8,10},{9,11},{10,... | collective-permute-start | bytes 2359304 | tf_op jit(solution)/shard_map/ppermute | solution.py:111
  45.4 14.2 %collective-permute-start.8 = (bf16[384,768]{1,0:T(8,128)(2,1)S(1)}, bf16[384,768]{1,0:T(8,128)(2,1)S(1)}, u32[]{:S(2)}, u32[]{:S(2)}) collective-permute-start(bf16[384,768]{1,0:T(8,128)(2,1)S(1)} %get-tuple-element.405.refs_2_), channel_id=1, source_target_pairs={{0,2},{1,3},{2,0},{3,1},{4,6},{5,7},{6,4},{7,5},{8,10},{9,11},{10,... | collective-permute-start | bytes 1769480 | tf_op jit(solution)/shard_map/ppermute | solution.py:111
  45.5 14.1 %collective-permute-start.9 = (bf16[384,384]{1,0:T(8,128)(2,1)S(1)}, bf16[384,384]{1,0:T(8,128)(2,1)S(1)}, u32[]{:S(2)}, u32[]{:S(2)}) collective-permute-start(bf16[384,384]{1,0:T(8,128)(2,1)S(1)} %get-tuple-element.395), channel_id=1, source_target_pairs={{0,1},{1,0},{2,3},{3,2},{4,5},{5,4},{6,7},{7,6},{8,9},{9,8},{10,11... | collective-permute-start | bytes 884744 | tf_op jit(solution)/shard_map/ppermute | solution.py:111
  47.2 16.5 %collective-permute-start.6 = (bf16[2,384,512]{2,1,0:T(8,128)(2,1)S(1)}, bf16[2,384,512]{2,1,0:T(8,128)(2,1)S(1)}, u32[]{:S(2)}, u32[]{:S(2)}) collective-permute-start(bf16[2,384,512]{2,1,0:T(8,128)(2,1)S(1)} %get-tuple-element.386), channel_id=1, source_target_pairs={{0,2},{1,3},{2,0},{3,1},{4,6},{5,7},{6,4},{7,5},{8,10},{9,11},{10,... | collective-permute-start | bytes 2359304 | tf_op jit(solution)/shard_map/ppermute | solution.py:111
  50.1 17.8 %collective-permute-start.5 = (bf16[8,64,768]{2,1,0:T(8,128)(2,1)S(1)}, bf16[8,64,768]{2,1,0:T(8,128)(2,1)S(1)}, u32[]{:S(2)}, u32[]{:S(2)}) collective-permute-start(bf16[8,64,768]{2,1,0:T(8,128)(2,1)S(1)} %get-tuple-element.384), channel_id=1, source_target_pairs={{0,4},{1,5},{2,3},{3,2},{4,0},{5,1},{6,7},{7,6},{8,12},{9,13},{10,... | collective-permute-start | bytes 2359304 | tf_op jit(solution)/shard_map/ppermute | solution.py:111
  63.1 16.3 %collective-permute-start.10 = (bf16[8,96,768]{2,1,0:T(8,128)(2,1)S(1)}, bf16[8,96,768]{2,1,0:T(8,128)(2,1)S(1)}, u32[]{:S(2)}, u32[]{:S(2)}) collective-permute-start(bf16[8,96,768]{2,1,0:T(8,128)(2,1)S(1)} %get-tuple-element.434), channel_id=1, source_target_pairs={{0,1},{1,0},{2,6},{3,7},{4,5},{5,4},{6,2},{7,3},{8,9},{9,8},{10,14... | collective-permute-start | bytes 3538952 | tf_op jit(solution)/shard_map/ppermute | solution.py:111
  66.2 23.4 %collective-permute-start.16 = (bf16[8,64,768]{2,1,0:T(8,128)(2,1)S(1)}, bf16[8,64,768]{2,1,0:T(8,128)(2,1)S(1)}, u32[]{:S(2)}, u32[]{:S(2)}) collective-permute-start(bf16[8,64,768]{2,1,0:T(8,128)(2,1)S(1)} %get-tuple-element.461), channel_id=1, source_target_pairs={{0,8},{1,9},{2,6},{3,7},{4,12},{5,13},{6,2},{7,3},{8,0},{9,1},{10,... | collective-permute-start | bytes 2359304 | tf_op jit(solution)/shard_map/ppermute | solution.py:111
  69.1 17.3 %collective-permute-start.12 = (bf16[4,64,768]{2,1,0:T(8,128)(2,1)S(1)}, bf16[4,64,768]{2,1,0:T(8,128)(2,1)S(1)}, u32[]{:S(2)}, u32[]{:S(2)}) collective-permute-start(bf16[4,64,768]{2,1,0:T(8,128)(2,1)S(1)} %add_convert_fusion.7), channel_id=1, source_target_pairs={{0,1},{1,0},{2,10},{3,11},{4,5},{5,4},{6,14},{7,15},{8,9},{9,8},{1... | collective-permute-start | bytes 1179656 | tf_op jit(solution)/shard_map/ppermute | solution.py:111
  79.5 9.9 %collective-permute-start.11 = (bf16[4,96,768]{2,1,0:T(8,128)(2,1)S(1)}, bf16[4,96,768]{2,1,0:T(8,128)(2,1)S(1)}, u32[]{:S(2)}, u32[]{:S(2)}) collective-permute-start(bf16[4,96,768]{2,1,0:T(8,128)(2,1)S(1)} %add_convert_fusion.1), channel_id=1, source_target_pairs={{0,8},{1,9},{2,3},{3,2},{4,12},{5,13},{6,7},{7,6},{8,0},{9,1},{10,... | collective-permute-start | bytes 1769480 | tf_op jit(solution)/shard_map/ppermute | solution.py:111
  86.4 5.7 %collective-permute-start.15 = (bf16[2,64,768]{2,1,0:T(8,128)(2,1)S(1)}, bf16[2,64,768]{2,1,0:T(8,128)(2,1)S(1)}, u32[]{:S(2)}, u32[]{:S(2)}) collective-permute-start(bf16[2,64,768]{2,1,0:T(8,128)(2,1)S(1)} %add_convert_fusion.23), channel_id=1, source_target_pairs={{0,8},{1,9},{2,6},{3,7},{4,12},{5,13},{6,2},{7,3},{8,0},{9,1},{10,... | collective-permute-start | bytes 589832 | tf_op jit(solution)/shard_map/ppermute | solution.py:111
  88.3 7.3 %collective-permute-start.14 = (bf16[8,48,1152]{2,1,0:T(8,128)(2,1)S(1)}, bf16[8,48,1152]{2,1,0:T(8,128)(2,1)S(1)}, u32[]{:S(2)}, u32[]{:S(2)}) collective-permute-start(bf16[8,48,1152]{2,1,0:T(8,128)(2,1)S(1)} %get-tuple-element.458), channel_id=1, source_target_pairs={{0,2},{1,3},{2,0},{3,1},{4,6},{5,7},{6,4},{7,5},{8,10},{9,11},{10,... | collective-permute-start | bytes 2654216 | tf_op jit(solution)/shard_map/ppermute | solution.py:111
  92.2 6.7 %collective-permute-start.13 = (bf16[2,96,768]{2,1,0:T(8,128)(2,1)S(1)}, bf16[2,96,768]{2,1,0:T(8,128)(2,1)S(1)}, u32[]{:S(2)}, u32[]{:S(2)}) collective-permute-start(bf16[2,96,768]{2,1,0:T(8,128)(2,1)S(1)} %add_convert_fusion.11), channel_id=1, source_target_pairs={{0,4},{1,5},{2,10},{3,11},{4,0},{5,1},{6,14},{7,15},{8,12},{9,13},... | collective-permute-start | bytes 884744 | tf_op jit(solution)/shard_map/ppermute | solution.py:111
  92.2 12.4 %collective-permute-start.19 = (bf16[4,64,768]{2,1,0:T(8,128)(2,1)S(1)}, bf16[4,64,768]{2,1,0:T(8,128)(2,1)S(1)}, u32[]{:S(2)}, u32[]{:S(2)}) collective-permute-start(bf16[4,64,768]{2,1,0:T(8,128)(2,1)S(1)} %add_convert_fusion.5), channel_id=1, source_target_pairs={{0,1},{1,0},{2,3},{3,2},{4,5},{5,4},{6,7},{7,6},{8,9},{9,8},{10,11... | collective-permute-start | bytes 1179656 | tf_op jit(solution)/shard_map/ppermute | solution.py:111
  93.0 11.7 %collective-permute-start.18 = (bf16[2,64,768]{2,1,0:T(8,128)(2,1)S(1)}, bf16[2,64,768]{2,1,0:T(8,128)(2,1)S(1)}, u32[]{:S(2)}, u32[]{:S(2)}) collective-permute-start(bf16[2,64,768]{2,1,0:T(8,128)(2,1)S(1)} %add_convert_fusion.21), channel_id=1, source_target_pairs={{0,16},{1,17},{2,18},{3,19},{4,20},{5,21},{6,22},{7,23},{8,24},{9,... | collective-permute-start | bytes 589832 | tf_op jit(solution)/shard_map/ppermute | solution.py:111
  95.8 8.7 %collective-permute-start.20 = (bf16[4,48,1152]{2,1,0:T(8,128)(2,1)S(1)}, bf16[4,48,1152]{2,1,0:T(8,128)(2,1)S(1)}, u32[]{:S(2)}, u32[]{:S(2)}) collective-permute-start(bf16[4,48,1152]{2,1,0:T(8,128)(2,1)S(1)} %add_convert_fusion.3), channel_id=1, source_target_pairs={{0,4},{1,5},{2,10},{3,11},{4,0},{5,1},{6,14},{7,15},{8,12},{9,13},... | collective-permute-start | bytes 1327112 | tf_op jit(solution)/shard_map/ppermute | solution.py:111
  101.6 14.9 %collective-permute-start.17 = (bf16[384,768]{1,0:T(8,128)(2,1)S(1)}, bf16[384,768]{1,0:T(8,128)(2,1)S(1)}, u32[]{:S(2)}, u32[]{:S(2)}) collective-permute-start(bf16[384,768]{1,0:T(8,128)(2,1)S(1)} %get-tuple-element.481), channel_id=1, source_target_pairs={{0,1},{1,0},{2,3},{3,2},{4,5},{5,4},{6,7},{7,6},{8,9},{9,8},{10,11... | collective-permute-start | bytes 1769480 | tf_op jit(solution)/shard_map/ppermute | solution.py:111
  102.0 21.7 %collective-permute-start.22 = (bf16[2,96,768]{2,1,0:T(8,128)(2,1)S(1)}, bf16[2,96,768]{2,1,0:T(8,128)(2,1)S(1)}, u32[]{:S(2)}, u32[]{:S(2)}) collective-permute-start(bf16[2,96,768]{2,1,0:T(8,128)(2,1)S(1)} %add_convert_fusion.9), channel_id=1, source_target_pairs={{0,16},{1,17},{2,18},{3,19},{4,20},{5,21},{6,22},{7,23},{8,24},{9,... | collective-permute-start | bytes 884744 | tf_op jit(solution)/shard_map/ppermute | solution.py:111
  104.8 19.5 %collective-permute-start.21 = (bf16[2,64,768]{2,1,0:T(8,128)(2,1)S(1)}, bf16[2,64,768]{2,1,0:T(8,128)(2,1)S(1)}, u32[]{:S(2)}, u32[]{:S(2)}) collective-permute-start(bf16[2,64,768]{2,1,0:T(8,128)(2,1)S(1)} %add_convert_fusion.18), channel_id=1, source_target_pairs={{0,8},{1,9},{2,6},{3,7},{4,12},{5,13},{6,2},{7,3},{8,0},{9,1},{10,... | collective-permute-start | bytes 589832 | tf_op jit(solution)/shard_map/ppermute | solution.py:111
  106.6 19.0 %collective-permute-start.24 = (bf16[2,48,1152]{2,1,0:T(8,128)(2,1)S(1)}, bf16[2,48,1152]{2,1,0:T(8,128)(2,1)S(1)}, u32[]{:S(2)}, u32[]{:S(2)}) collective-permute-start(bf16[2,48,1152]{2,1,0:T(8,128)(2,1)S(1)} %add_convert_fusion.15), channel_id=1, source_target_pairs={{0,8},{1,9},{2,18},{3,19},{4,12},{5,13},{6,22},{7,23},{8,0},{9,1},... | collective-permute-start | bytes 663560 | tf_op jit(solution)/shard_map/ppermute | solution.py:111
  106.9 25.6 %collective-permute-start.26 = (bf16[2,64,768]{2,1,0:T(8,128)(2,1)S(1)}, bf16[2,64,768]{2,1,0:T(8,128)(2,1)S(1)}, u32[]{:S(2)}, u32[]{:S(2)}) collective-permute-start(bf16[2,64,768]{2,1,0:T(8,128)(2,1)S(1)} %add_convert_fusion.20), channel_id=1, source_target_pairs={{0,4},{1,5},{2,18},{3,19},{4,0},{5,1},{6,22},{7,23},{8,12},{9,13},... | collective-permute-start | bytes 589832 | tf_op jit(solution)/shard_map/ppermute | solution.py:111
  123.8 8.7 %collective-permute-start.27 = (bf16[2,96,768]{2,1,0:T(8,128)(2,1)S(1)}, bf16[2,96,768]{2,1,0:T(8,128)(2,1)S(1)}, u32[]{:S(2)}, u32[]{:S(2)}) collective-permute-start(bf16[2,96,768]{2,1,0:T(8,128)(2,1)S(1)} %add_convert_fusion.8), channel_id=1, source_target_pairs={{0,4},{1,5},{2,10},{3,11},{4,0},{5,1},{6,14},{7,15},{8,12},{9,13},... | collective-permute-start | bytes 884744 | tf_op jit(solution)/shard_map/ppermute | solution.py:111
  124.3 12.4 %collective-permute-start.23 = (bf16[4,64,768]{2,1,0:T(8,128)(2,1)S(1)}, bf16[4,64,768]{2,1,0:T(8,128)(2,1)S(1)}, u32[]{:S(2)}, u32[]{:S(2)}) collective-permute-start(bf16[4,64,768]{2,1,0:T(8,128)(2,1)S(1)} %constant_dynamic-update-slice_fusion), channel_id=1, source_target_pairs={{0,1},{1,0},{2,10},{3,11},{4,5},{5,4},{6,14},{7,15},{8,9},{9,8},{1... | collective-permute-start | bytes 1179656 | tf_op jit(solution)/shard_map/ppermute | solution.py:111
  125.6 10.0 %collective-permute-start.25 = (bf16[2,48,1152]{2,1,0:T(8,128)(2,1)S(1)}, bf16[2,48,1152]{2,1,0:T(8,128)(2,1)S(1)}, u32[]{:S(2)}, u32[]{:S(2)}) collective-permute-start(bf16[2,48,1152]{2,1,0:T(8,128)(2,1)S(1)} %add_convert_fusion.13), channel_id=1, source_target_pairs={{0,16},{1,17},{2,6},{3,7},{4,20},{5,21},{6,2},{7,3},{8,24},{9,25},... | collective-permute-start | bytes 663560 | tf_op jit(solution)/shard_map/ppermute | solution.py:111
  132.5 14.2 %collective-permute-start.31 = (bf16[4,96,768]{2,1,0:T(8,128)(2,1)S(1)}, bf16[4,96,768]{2,1,0:T(8,128)(2,1)S(1)}, u32[]{:S(2)}, u32[]{:S(2)}) collective-permute-start(bf16[4,96,768]{2,1,0:T(8,128)(2,1)S(1)} %constant_dynamic-update-slice_fusion.2), channel_id=1, source_target_pairs={{0,8},{1,9},{2,3},{3,2},{4,12},{5,13},{6,7},{7,6},{8,0},{9,1},{10,... | collective-permute-start | bytes 1769480 | tf_op jit(solution)/shard_map/ppermute | solution.py:111
  132.7 15.8 %collective-permute-start.30 = (bf16[2,64,768]{2,1,0:T(8,128)(2,1)S(1)}, bf16[2,64,768]{2,1,0:T(8,128)(2,1)S(1)}, u32[]{:S(2)}, u32[]{:S(2)}) collective-permute-start(bf16[2,64,768]{2,1,0:T(8,128)(2,1)S(1)} %add_convert_fusion.17), channel_id=1, source_target_pairs={{0,16},{1,17},{2,10},{3,11},{4,20},{5,21},{6,14},{7,15},{8,24},{9,... | collective-permute-start | bytes 589832 | tf_op jit(solution)/shard_map/ppermute | solution.py:111
  135.7 8.4 %collective-permute-start.32 = (bf16[2,48,1152]{2,1,0:T(8,128)(2,1)S(1)}, bf16[2,48,1152]{2,1,0:T(8,128)(2,1)S(1)}, u32[]{:S(2)}, u32[]{:S(2)}) collective-permute-start(bf16[2,48,1152]{2,1,0:T(8,128)(2,1)S(1)} %add_convert_fusion.12), channel_id=1, source_target_pairs={{0,1},{1,0},{2,3},{3,2},{4,5},{5,4},{6,7},{7,6},{8,9},{9,8},{10,11... | collective-permute-start | bytes 663560 | tf_op jit(solution)/shard_map/ppermute | solution.py:111
  136.8 11.7 %collective-permute-start.29 = (bf16[8,64,768]{2,1,0:T(8,128)(2,1)S(1)}, bf16[8,64,768]{2,1,0:T(8,128)(2,1)S(1)}, u32[]{:S(2)}, u32[]{:S(2)}) collective-permute-start(bf16[8,64,768]{2,1,0:T(8,128)(2,1)S(1)} %constant_dynamic-update-slice_fusion.4.own), channel_id=1, source_target_pairs={{0,2},{1,3},{2,0},{3,1},{4,6},{5,7},{6,4},{7,5},{8,10},{9,11},{10,... | collective-permute-start | bytes 2359304 | tf_op jit(solution)/shard_map/ppermute | solution.py:111
  136.9 14.0 %collective-permute-start.28 = (bf16[8,64,768]{2,1,0:T(8,128)(2,1)S(1)}, bf16[8,64,768]{2,1,0:T(8,128)(2,1)S(1)}, u32[]{:S(2)}, u32[]{:S(2)}) collective-permute-start(bf16[8,64,768]{2,1,0:T(8,128)(2,1)S(1)} %constant_dynamic-update-slice_fusion.4.own), channel_id=1, source_target_pairs={{0,4},{1,5},{2,3},{3,2},{4,0},{5,1},{6,7},{7,6},{8,12},{9,13},{10,... | collective-permute-start | bytes 2359304 | tf_op jit(solution)/shard_map/ppermute | solution.py:111
  144.2 12.9 %collective-permute-start.35 = (bf16[2,48,2304]{2,1,0:T(8,128)(2,1)S(1)}, bf16[2,48,2304]{2,1,0:T(8,128)(2,1)S(1)}, u32[]{:S(2)}, u32[]{:S(2)}) collective-permute-start(bf16[2,48,2304]{2,1,0:T(8,128)(2,1)S(1)} %constant_dynamic-update-slice_fusion.6), channel_id=1, source_target_pairs={{0,8},{1,9},{2,18},{3,19},{4,12},{5,13},{6,22},{7,23},{8,0},{9,1},... | collective-permute-start | bytes 1327112 | tf_op jit(solution)/shard_map/ppermute | solution.py:111
  146.8 19.8 %collective-permute-start.39 = (bf16[8,96,768]{2,1,0:T(8,128)(2,1)S(1)}, bf16[8,96,768]{2,1,0:T(8,128)(2,1)S(1)}, u32[]{:S(2)}, u32[]{:S(2)}) collective-permute-start(bf16[8,96,768]{2,1,0:T(8,128)(2,1)S(1)} %constant_dynamic-update-slice_fusion.8.own), channel_id=1, source_target_pairs={{0,1},{1,0},{2,6},{3,7},{4,5},{5,4},{6,2},{7,3},{8,9},{9,8},{10,14... | collective-permute-start | bytes 3538952 | tf_op jit(solution)/shard_map/ppermute | solution.py:111
  148.5 19.0 %collective-permute-start.38 = (bf16[8,96,768]{2,1,0:T(8,128)(2,1)S(1)}, bf16[8,96,768]{2,1,0:T(8,128)(2,1)S(1)}, u32[]{:S(2)}, u32[]{:S(2)}) collective-permute-start(bf16[8,96,768]{2,1,0:T(8,128)(2,1)S(1)} %constant_dynamic-update-slice_fusion.8.own), channel_id=1, source_target_pairs={{0,2},{1,3},{2,0},{3,1},{4,6},{5,7},{6,4},{7,5},{8,10},{9,11},{10,... | collective-permute-start | bytes 3538952 | tf_op jit(solution)/shard_map/ppermute | solution.py:111
  148.5 11.4 %collective-permute-start.34 = (bf16[2,64,768]{2,1,0:T(8,128)(2,1)S(1)}, bf16[2,64,768]{2,1,0:T(8,128)(2,1)S(1)}, u32[]{:S(2)}, u32[]{:S(2)}) collective-permute-start(bf16[2,64,768]{2,1,0:T(8,128)(2,1)S(1)} %add_convert_fusion.16), channel_id=1, source_target_pairs={{0,4},{1,5},{2,18},{3,19},{4,0},{5,1},{6,22},{7,23},{8,12},{9,13},... | collective-permute-start | bytes 589832 | tf_op jit(solution)/shard_map/ppermute | solution.py:111
  157.1 4.4 %collective-permute-start.33 = (bf16[8,64,768]{2,1,0:T(8,128)(2,1)S(1)}, bf16[8,64,768]{2,1,0:T(8,128)(2,1)S(1)}, u32[]{:S(2)}, u32[]{:S(2)}) collective-permute-start(bf16[8,64,768]{2,1,0:T(8,128)(2,1)S(1)} %collective-permute-done.28.own), channel_id=1, source_target_pairs={{0,2},{1,3},{2,0},{3,1},{4,6},{5,7},{6,4},{7,5},{8,10},{9,11},{10,... | collective-permute-start | bytes 2359304 | tf_op jit(solution)/shard_map/ppermute | solution.py:111
  157.2 16.0 %collective-permute-start.36 = (bf16[4,48,2304]{2,1,0:T(8,128)(2,1)S(1)}, bf16[4,48,2304]{2,1,0:T(8,128)(2,1)S(1)}, u32[]{:S(2)}, u32[]{:S(2)}) collective-permute-start(bf16[4,48,2304]{2,1,0:T(8,128)(2,1)S(1)} %constant_dynamic-update-slice_fusion.10.own), channel_id=1, source_target_pairs={{0,4},{1,5},{2,10},{3,11},{4,0},{5,1},{6,14},{7,15},{8,12},{9,13},... | collective-permute-start | bytes 2654216 | tf_op jit(solution)/shard_map/ppermute | solution.py:111
  160.0 13.0 %collective-permute-start.37 = (bf16[4,64,768]{2,1,0:T(8,128)(2,1)S(1)}, bf16[4,64,768]{2,1,0:T(8,128)(2,1)S(1)}, u32[]{:S(2)}, u32[]{:S(2)}) collective-permute-start(bf16[4,64,768]{2,1,0:T(8,128)(2,1)S(1)} %constant_dynamic-update-slice_fusion.12), channel_id=1, source_target_pairs={{0,1},{1,0},{2,3},{3,2},{4,5},{5,4},{6,7},{7,6},{8,9},{9,8},{10,11... | collective-permute-start | bytes 1179656 | tf_op jit(solution)/shard_map/ppermute | solution.py:111
  166.5 8.1 %collective-permute-start.42 = (bf16[8,96,768]{2,1,0:T(8,128)(2,1)S(1)}, bf16[8,96,768]{2,1,0:T(8,128)(2,1)S(1)}, u32[]{:S(2)}, u32[]{:S(2)}) collective-permute-start(bf16[8,96,768]{2,1,0:T(8,128)(2,1)S(1)} %collective-permute-done.39.own), channel_id=1, source_target_pairs={{0,2},{1,3},{2,0},{3,1},{4,6},{5,7},{6,4},{7,5},{8,10},{9,11},{10,... | collective-permute-start | bytes 3538952 | tf_op jit(solution)/shard_map/ppermute | solution.py:111
  167.4 7.3 %collective-permute-start.41 = (bf16[4,48,2304]{2,1,0:T(8,128)(2,1)S(1)}, bf16[4,48,2304]{2,1,0:T(8,128)(2,1)S(1)}, u32[]{:S(2)}, u32[]{:S(2)}) collective-permute-start(bf16[4,48,2304]{2,1,0:T(8,128)(2,1)S(1)} %constant_dynamic-update-slice_fusion.10.own), channel_id=1, source_target_pairs={{0,2},{1,3},{2,0},{3,1},{4,6},{5,7},{6,4},{7,5},{8,10},{9,11},{10,... | collective-permute-start | bytes 2654216 | tf_op jit(solution)/shard_map/ppermute | solution.py:111
  173.2 7.8 %collective-permute-start.40 = (bf16[4,48,2304]{2,1,0:T(8,128)(2,1)S(1)}, bf16[4,48,2304]{2,1,0:T(8,128)(2,1)S(1)}, u32[]{:S(2)}, u32[]{:S(2)}) collective-permute-start(bf16[4,48,2304]{2,1,0:T(8,128)(2,1)S(1)} %collective-permute-done.36.own), channel_id=1, source_target_pairs={{0,2},{1,3},{2,0},{3,1},{4,6},{5,7},{6,4},{7,5},{8,10},{9,11},{10,... | collective-permute-start | bytes 2654216 | tf_op jit(solution)/shard_map/ppermute | solution.py:111
  173.2 12.0 %collective-permute-start.43 = (bf16[8,64,768]{2,1,0:T(8,128)(2,1)S(1)}, bf16[8,64,768]{2,1,0:T(8,128)(2,1)S(1)}, u32[]{:S(2)}, u32[]{:S(2)}) collective-permute-start(bf16[8,64,768]{2,1,0:T(8,128)(2,1)S(1)} %constant_dynamic-update-slice_fusion.14.own), channel_id=1, source_target_pairs={{0,8},{1,9},{2,6},{3,7},{4,12},{5,13},{6,2},{7,3},{8,0},{9,1},{10,... | collective-permute-start | bytes 2359304 | tf_op jit(solution)/shard_map/ppermute | solution.py:111
  173.7 11.5 %collective-permute-start.45 = (bf16[8,64,768]{2,1,0:T(8,128)(2,1)S(1)}, bf16[8,64,768]{2,1,0:T(8,128)(2,1)S(1)}, u32[]{:S(2)}, u32[]{:S(2)}) collective-permute-start(bf16[8,64,768]{2,1,0:T(8,128)(2,1)S(1)} %constant_dynamic-update-slice_fusion.14.own), channel_id=1, source_target_pairs={{0,2},{1,3},{2,0},{3,1},{4,6},{5,7},{6,4},{7,5},{8,10},{9,11},{10,... | collective-permute-start | bytes 2359304 | tf_op jit(solution)/shard_map/ppermute | solution.py:111
  185.2 3.3 %collective-permute-start.44 = (bf16[8,64,768]{2,1,0:T(8,128)(2,1)S(1)}, bf16[8,64,768]{2,1,0:T(8,128)(2,1)S(1)}, u32[]{:S(2)}, u32[]{:S(2)}) collective-permute-start(bf16[8,64,768]{2,1,0:T(8,128)(2,1)S(1)} %collective-permute-done.43.own), channel_id=1, source_target_pairs={{0,2},{1,3},{2,0},{3,1},{4,6},{5,7},{6,4},{7,5},{8,10},{9,11},{10,... | collective-permute-start | bytes 2359304 | tf_op jit(solution)/shard_map/ppermute | solution.py:111
  (18 other events, 100.0 us)
where the time goes:
time: 193 us
  Pallas kernels  94.1 us (49%)
  waiting for transfers between devices  48.9 us (25%)
  starting transfers between devices  41.8 us (22%)
  local copies, waits for them, and re-layouts  3.38 us (2%)
  other arithmetic  3.09 us (2%)
    pallas_call x26, Pallas kernels, call(): pl.pallas_call(kernel, grid_spec=pltpu.PrefetchScalarGridSpec(num_scalar_...  94.1 us
    ppermute x46, waiting for transfers between devices, swap(): return lax.ppermute(array, AXES, pairs)  48.9 us
    ppermute x46, starting transfers between devices, swap(): return lax.ppermute(array, AXES, pairs)  41.8 us
  transfers between devices with their start and end apart: 46, of which 16 were waited for; matrix products, arithmetic and copies ran while one was open for 2% of the time, Pallas kernels for 42%

commit v1 on v0

--- a/solution.py
+++ b/solution.py
@@ -839,7 +839,8 @@
     half = width // 2
     freqs = jnp.exp(jnp.arange(half, dtype=f32) * (-math.log(10000.0) / half))[None]
     pos = run(functools.partial(positions, scalars), visible, freqs)
-    normed1, qkv, resid = run(functools.partial(ln_qkv, scalars, False), tok, pos, gain1, w_qkv)
+    w_first = pltpu.with_memory_space_constraint(w_qkv, pltpu.HBM)
+    normed1, qkv, resid = run(functools.partial(ln_qkv, scalars, False), tok, pos, gain1, w_first)
     sums = run(functools.partial(attention, scalars), qkv, qkv)
     pos_far = run(functools.partial(positions, scalars), vis_far, freqs)
     normed1_far, kv_far = run(functools.partial(ln_qkv, scalars, True), tok_far, pos_far, gain1, w_qkv)

time: 193 us -> 193 us (level)
  local copies, waits for them, and re-layouts: 3.38 us -> 1.38 us
    unnamed x48 -> x46, local copies, waits for them, and re-layouts: 2.96 us -> 0.97 us
  transfers between devices with their start and end apart: 46 -> 46, of which waited for: 16 -> 16; matrix products, arithmetic and copies ran while one was open for 2% -> 2% of each run, Pallas kernels for 42% -> 43%
where the time goes in v1:
time: 193 us
  Pallas kernels  95.7 us (50%)
  waiting for transfers between devices  49.3 us (26%)
  starting transfers between devices  41.8 us (22%)
  other arithmetic  3.09 us (2%)
    pallas_call x26, Pallas kernels, call(): pl.pallas_call(kernel, grid_spec=pltpu.PrefetchScalarGridSpec(num_scalar_...  95.7 us
    ppermute x46, waiting for transfers between devices, swap(): return lax.ppermute(array, AXES, pairs)  49.3 us
    ppermute x46, starting transfers between devices, swap(): return lax.ppermute(array, AXES, pairs)  41.8 us
  transfers between devices with their start and end apart: 46, of which 16 were waited for; matrix products, arithmetic and copies ran while one was open for 2% of the time, Pallas kernels for 43%

profile of v1, /device:TPU:0, one launch (start us, length us, event | category | flops | bytes accessed | tf_op | source)
XLA Modules:
  0.0 192.6 jit_solution(16639725197388973409)
XLA Ops:
  0.6 3.0 %collective-permute-start = (bf16[384,768]{1,0:T(8,128)(2,1)}, bf16[384,768]{1,0:T(8,128)(2,1)}, u32[]{:S(2)}, u32[]{:S(2)}) collective-permute-start(bf16[384,768]{1,0:T(8,128)(2,1)} %bitcast.22), channel_id=1, source_target_pairs={{0,1},{1,0},{2,3},{3,2},{4,5},{5,4},{6,7},{7,6},{8,9},{9,8},{10,11... | collective-permute-start | bytes 1769480 | tf_op jit(solution)/shard_map/ppermute | solution.py:111
  6.1 4.8 %shard_map.153 = (bf16[384,768]{1,0:T(8,128)(2,1)S(1)}, bf16[384,2304]{1,0:T(8,128)(2,1)S(1)}, f32[384,768]{1,0:T(8,128)S(1)}) custom-call(s32[10]{0:T(128)S(1)} %stack.37.s, bf16[384,768]{1,0:T(8,128)(2,1)S(1)} %bitcast.23, f32[384,768]{1,0:T(8,128)S(1)} %shard_map.152.pos, f32[1,768]{1,0:T(1,128)S(1)} %broadcast_in_dim.16.gain, bf16[768,2304]{1,0:T(8,128)(2,1)} %w.17), custom_call_target="tpu_custom_call" | custom-call | flops 1 | bytes 1 | tf_op jit(solution)/shard_map/pallas_call | solution.py:54
  11.0 4.4 %shard_map.154 = (f32[6,128,384]{2,1,0:T(8,128)S(1)}, f32[6,8,768]{2,1,0:T(8,128)S(1)}) custom-call(s32[10]{0:T(128)S(1)} %stack.37.s, bf16[384,2304]{1,0:T(8,128)(2,1)S(1)} %get-tuple-element.426.q.k.v.k_o.v_o, bf16[384,2304]{1,0:T(8,128)(2,1)S(1)} %get-tuple-element.426.q.k.v.k_o.v_o, bf16[384,2304]{1,0:T(8,128)(2,1)S(1)} %get-tuple-element.426.q.k.v.k_o.v_o), custom_call_target="tpu_custom_call" | custom-call | flops 1 | bytes 1 | tf_op jit(solution)/shard_map/pallas_call | solution.py:54
  15.4 1.9 collective-permute-done.1.visible
  18.9 3.5 %shard_map.156 = (bf16[384,768]{1,0:T(8,128)(2,1)S(1)}, bf16[384,1536]{1,0:T(8,128)(2,1)S(1)}) custom-call(s32[10]{0:T(128)S(1)} %stack.37.s, bf16[384,768]{1,0:T(8,128)(2,1)} %collective-permute-done.tok, f32[384,768]{1,0:T(8,128)S(1)} %shard_map.155.pos, f32[1,768]{1,0:T(1,128)S(1)} %broadcast_in_dim.16.gain, bf16[768,2304]{1,0:T(8,128)(2,1)S(1)} %copy-done), custom_call_target="tpu_custom_call" | custom-call | flops 1 | bytes 1 | tf_op jit(solution)/shard_map/pallas_call | solution.py:54
  22.4 4.6 %shard_map.157.att.att_half.refs_0_ = bf16[384,768]{1,0:T(8,128)(2,1)S(1)} custom-call(s32[10]{0:T(128)S(1)} %stack.37.s, bf16[384,2304]{1,0:T(8,128)(2,1)S(1)} %get-tuple-element.426.q.k.v.k_o.v_o, bf16[384,1536]{1,0:T(8,128)(2,1)S(1)} %get-tuple-element.427.k.v.k_f.v_f, bf16[384,1536]{1,0:T(8,128)(2,1)S(1)} %get-tuple-element.427.k.v.k_f.v_f, ...), custom_call_target="tpu_custom_call" | custom-call | flops 1 | bytes 1 | tf_op jit(solution)/shard_map/pallas_call | solution.py:54
  27.1 1.6 shard_map.158
  29.4 4.5 %shard_map.159 = (bf16[2,384,512]{2,1,0:T(8,128)(2,1)S(1)}, bf16[2,384,512]{2,1,0:T(8,128)(2,1)S(1)}, f32[384,768]{1,0:T(8,128)S(1)}, f32[384,768]{1,0:T(8,128)S(1)}) custom-call(s32[10]{0:T(128)S(1)} %stack.37.s, bf16[384,768]{1,0:T(8,128)(2,1)S(1)} %get-tuple-element.354.normed, bf16[384,768]{1,0:T(8,128)(2,1)S(1)} %bitcast.17, ...), custom_call_target="tpu_custom_call" | custom-call | flops 1 | bytes 1 | tf_op jit(solution)/shard_map/pallas_call | solution.py:54
  34.1 10.9 %shard_map.160 = (bf16[2,384,512]{2,1,0:T(8,128)(2,1)S(1)}, bf16[2,384,512]{2,1,0:T(8,128)(2,1)S(1)}, bf16[2,384,512]{2,1,0:T(8,128)(2,1)S(1)}, bf16[2,384,512]{...) custom-call(s32[10]{0:T(128)S(1)} %stack.37.s, ...), custom_call_target="tpu_custom_call" | custom-call | flops 1 | bytes 1 | tf_op jit(solution)/shard_map/pallas_call | solution.py:54
  45.5 1.7 collective-permute-start.9
  47.4 2.7 %shard_map.161 = (bf16[8,64,768]{2,1,0:T(8,128)(2,1)S(1)}, bf16[8,64,768]{2,1,0:T(8,128)(2,1)S(1)}) custom-call(s32[10]{0:T(128)S(1)} %stack.37.s, bf16[2,384,512]{2,1,0:T(8,128)(2,1)S(1)} %get-tuple-element.371.act.grad, bf16[2,384,512]{2,1,0:T(8,128)(2,1)S(1)} %collective-permute-done.4.act_o.grad_o, bf16[2,384,512]{2,1,0:T(8,128)(2,1)S(1)} %get-tuple-element.371.act.grad, ...), custom_call_target="tpu_custom_call" | custom-call | flops 1 | bytes 1 | tf_op jit(solution)/shard_map/pallas_call | solution.py:54
  50.1 1.6 collective-permute-start.5
  51.6 7.9 %shard_map.162 = (bf16[384,384]{1,0:T(8,128)(2,1)S(1)}, f32[768,384]{1,0:T(8,128)S(1)}, f32[768,384]{1,0:T(8,128)S(1)}) custom-call(s32[10]{0:T(128)S(1)} %stack.37.s, bf16[384,2304]{1,0:T(8,128)(2,1)S(1)} %get-tuple-element.426.q.k.v.k_o.v_o, bf16[384,384]{1,0:T(8,128)(2,1)S(1)} %get-tuple-element.379.g, ...), custom_call_target="tpu_custom_call" | custom-call | flops 1 | bytes 1 | tf_op jit(solution)/shard_map/pallas_call | solution.py:54
  59.6 3.5 %shard_map.163 = (bf16[8,96,768]{2,1,0:T(8,128)(2,1)S(1)}, bf16[8,96,768]{2,1,0:T(8,128)(2,1)S(1)}) custom-call(s32[10]{0:T(128)S(1)} %stack.37.s, bf16[2,384,512]{2,1,0:T(8,128)(2,1)S(1)} %get-tuple-element.397.act.grad, bf16[2,384,512]{2,1,0:T(8,128)(2,1)S(1)} %collective-permute-done.7.act_o.grad_o, bf16[2,384,512]{2,1,0:T(8,128)(2,1)S(1)} %get-tuple-element.397.act.grad, ...), custom_call_target="tpu_custom_call" | custom-call | flops 1 | bytes 1 | tf_op jit(solution)/shard_map/pallas_call | solution.py:54
  63.7 2.5 %shard_map.164 = (bf16[8,64,768]{2,1,0:T(8,128)(2,1)S(1)}, bf16[8,64,768]{2,1,0:T(8,128)(2,1)S(1)}) custom-call(s32[10]{0:T(128)S(1)} %stack.37.s, bf16[2,384,512]{2,1,0:T(8,128)(2,1)S(1)} %get-tuple-element.409.act.grad, bf16[2,384,512]{2,1,0:T(8,128)(2,1)S(1)} %collective-permute-done.6.act_o.grad_o, bf16[2,384,512]{2,1,0:T(8,128)(2,1)S(1)} %get-tuple-element.409.act.grad, ...), custom_call_target="tpu_custom_call" | custom-call | flops 1 | bytes 1 | tf_op jit(solution)/shard_map/pallas_call | solution.py:54
  66.2 1.6 collective-permute-start.16
  69.1 1.6 collective-permute-start.12
  70.7 8.4 %shard_map.166 = (bf16[384,384]{1,0:T(8,128)(2,1)S(1)}, bf16[768,384]{1,0:T(8,128)(2,1)S(1)}, bf16[768,384]{1,0:T(8,128)(2,1)S(1)}) custom-call(s32[10]{0:T(128)S(1)} %stack.37.s, bf16[384,384]{1,0:T(8,128)(2,1)S(1)} %shard_map.165.q, bf16[384,384]{1,0:T(8,128)(2,1)S(1)} %collective-permute-done.9.g, bf16[384,2304]{1,0:T(8,128)(2,1)S(1)} %get-tuple-element.426.q.k.v.k_o.v_o, ...), custom_call_target="tpu_custom_call" | custom-call | flops 1 | bytes 1 | tf_op jit(solution)/shard_map/pallas_call | solution.py:54
  79.5 1.6 collective-permute-start.11
  81.3 3.4 %shard_map.167 = (bf16[8,48,1152]{2,1,0:T(8,128)(2,1)S(1)}, bf16[8,48,1152]{2,1,0:T(8,128)(2,1)S(1)}) custom-call(s32[10]{0:T(128)S(1)} %stack.37.s, bf16[384,768]{1,0:T(8,128)(2,1)S(1)} %get-tuple-element.441.n_own, bf16[384,768]{1,0:T(8,128)(2,1)S(1)} %copy-done.8, bf16[384,384]{1,0:T(8,128)(2,1)S(1)} %get-tuple-element.474.gq_o, ...), custom_call_target="tpu_custom_call" | custom-call | flops 1 | bytes 1 | tf_op jit(solution)/shard_map/pallas_call | solution.py:54
  84.7 1.7 collective-permute-done.12
  86.4 1.9 collective-permute-start.15
  89.8 2.3 %collective-permute-done.15 = bf16[2,64,768]{2,1,0:T(8,128)(2,1)S(1)} collective-permute-done((bf16[2,64,768]{2,1,0:T(8,128)(2,1)S(1)}, bf16[2,64,768]{2,1,0:T(8,128)(2,1)S(1)}, u32[]{:S(2)}, u32[]{:S(2)}) %collective-permute-start.15) | collective-permute-done | bytes 196640 | tf_op jit(solution)/shard_map/ppermute | solution.py:111
  93.0 2.7 %collective-permute-start.18 = (bf16[2,64,768]{2,1,0:T(8,128)(2,1)S(1)}, bf16[2,64,768]{2,1,0:T(8,128)(2,1)S(1)}, u32[]{:S(2)}, u32[]{:S(2)}) collective-permute-start(bf16[2,64,768]{2,1,0:T(8,128)(2,1)S(1)} %add_convert_fusion.21), channel_id=1, source_target_pairs={{0,16},{1,17},{2,18},{3,19},{4,20},{5,21},{6,22},{7,23},{8,24},{9,... | collective-permute-start | bytes 589832 | tf_op jit(solution)/shard_map/ppermute | solution.py:111
  99.0 2.6 %shard_map.168 = (f32[384,768]{1,0:T(8,128)S(1)}, bf16[384,768]{1,0:T(8,128)(2,1)S(1)}) custom-call(s32[10]{0:T(128)S(1)} %stack.37.s, bf16[384,384]{1,0:T(8,128)(2,1)S(1)} %get-tuple-element.474.gq_o, bf16[384,384]{1,0:T(8,128)(2,1)S(1)} %get-tuple-element.475.gq_f, bf16[768,384]{1,0:T(8,128)(2,1)S(1)} %get-tuple-element.476.gk, ...), custom_call_target="tpu_custom_call" | custom-call | flops 1 | bytes 1 | tf_op jit(solution)/shard_map/pallas_call | solution.py:54
  102.0 2.5 %collective-permute-start.22 = (bf16[2,96,768]{2,1,0:T(8,128)(2,1)S(1)}, bf16[2,96,768]{2,1,0:T(8,128)(2,1)S(1)}, u32[]{:S(2)}, u32[]{:S(2)}) collective-permute-start(bf16[2,96,768]{2,1,0:T(8,128)(2,1)S(1)} %add_convert_fusion.9), channel_id=1, source_target_pairs={{0,16},{1,17},{2,18},{3,19},{4,20},{5,21},{6,22},{7,23},{8,24},{9,... | collective-permute-start | bytes 884744 | tf_op jit(solution)/shard_map/ppermute | solution.py:111
  104.8 1.8 collective-permute-start.21
  108.0 8.4 %collective-permute-done.17.far = bf16[384,768]{1,0:T(8,128)(2,1)S(1)} collective-permute-done((bf16[384,768]{1,0:T(8,128)(2,1)S(1)}, bf16[384,768]{1,0:T(8,128)(2,1)S(1)}, u32[]{:S(2)}, u32[]{:S(2)}) %collective-permute-start.17) | collective-permute-done | bytes 589856 | tf_op jit(solution)/shard_map/ppermute | solution.py:111
  116.4 7.3 %collective-permute-done.22 = bf16[2,96,768]{2,1,0:T(8,128)(2,1)S(1)} collective-permute-done((bf16[2,96,768]{2,1,0:T(8,128)(2,1)S(1)}, bf16[2,96,768]{2,1,0:T(8,128)(2,1)S(1)}, u32[]{:S(2)}, u32[]{:S(2)}) %collective-permute-start.22) | collective-permute-done | bytes 294944 | tf_op jit(solution)/shard_map/ppermute | solution.py:111
  125.7 6.8 %collective-permute-done.27 = bf16[2,96,768]{2,1,0:T(8,128)(2,1)S(1)} collective-permute-done((bf16[2,96,768]{2,1,0:T(8,128)(2,1)S(1)}, bf16[2,96,768]{2,1,0:T(8,128)(2,1)S(1)}, u32[]{:S(2)}, u32[]{:S(2)}) %collective-permute-start.27) | collective-permute-done | bytes 294944 | tf_op jit(solution)/shard_map/ppermute | solution.py:111
  132.7 2.9 %collective-permute-start.30 = (bf16[2,64,768]{2,1,0:T(8,128)(2,1)S(1)}, bf16[2,64,768]{2,1,0:T(8,128)(2,1)S(1)}, u32[]{:S(2)}, u32[]{:S(2)}) collective-permute-start(bf16[2,64,768]{2,1,0:T(8,128)(2,1)S(1)} %add_convert_fusion.17), channel_id=1, source_target_pairs={{0,16},{1,17},{2,10},{3,11},{4,20},{5,21},{6,14},{7,15},{8,24},{9,... | collective-permute-start | bytes 589832 | tf_op jit(solution)/shard_map/ppermute | solution.py:111
  137.5 6.6 %collective-permute-done.32 = bf16[2,48,1152]{2,1,0:T(8,128)(2,1)S(1)} collective-permute-done((bf16[2,48,1152]{2,1,0:T(8,128)(2,1)S(1)}, bf16[2,48,1152]{2,1,0:T(8,128)(2,1)S(1)}, u32[]{:S(2)}, u32[]{:S(2)}) %collective-permute-start.32) | collective-permute-done | bytes 221216 | tf_op jit(solution)/shard_map/ppermute | solution.py:111
  144.2 2.4 %collective-permute-done.31 = bf16[4,96,768]{2,1,0:T(8,128)(2,1)S(1)} collective-permute-done((bf16[4,96,768]{2,1,0:T(8,128)(2,1)S(1)}, bf16[4,96,768]{2,1,0:T(8,128)(2,1)S(1)}, u32[]{:S(2)}, u32[]{:S(2)}) %collective-permute-start.31) | collective-permute-done | bytes 589856 | tf_op jit(solution)/shard_map/ppermute | solution.py:111
  146.8 1.7 collective-permute-start.39
  149.1 1.8 collective-permute-done.28.own
  151.0 2.6 %shard_map.169 = (f32[2,2,8,384]{3,2,1,0:T(8,128)S(1)}, f32[3072,768]{1,0:T(8,128)}, f32[768,3072]{1,0:T(8,128)}) custom-call(s32[10]{0:T(128)S(1)} %stack.37.s, bf16[8,64,768]{2,1,0:T(8,128)(2,1)S(1)} %constant_dynamic-update-slice_fusion.4.own, bf16[8,64,768]{2,1,0:T(8,128)(2,1)S(1)} %collective-permute-done.29.other, ...), custom_call_target="tpu_custom_call", output_to_operand_aliasing={{0}: (4, {})} | custom-call | flops 1 | bytes 1 | tf_op jit(solution)/shard_map/pallas_call | solution.py:54
  153.6 3.5 %collective-permute-done.35 = bf16[2,48,2304]{2,1,0:T(8,128)(2,1)S(1)} collective-permute-done((bf16[2,48,2304]{2,1,0:T(8,128)(2,1)S(1)}, bf16[2,48,2304]{2,1,0:T(8,128)(2,1)S(1)}, u32[]{:S(2)}, u32[]{:S(2)}) %collective-permute-start.35) | collective-permute-done | bytes 442400 | tf_op jit(solution)/shard_map/ppermute | solution.py:111
  157.2 2.7 %collective-permute-start.36 = (bf16[4,48,2304]{2,1,0:T(8,128)(2,1)S(1)}, bf16[4,48,2304]{2,1,0:T(8,128)(2,1)S(1)}, u32[]{:S(2)}, u32[]{:S(2)}) collective-permute-start(bf16[4,48,2304]{2,1,0:T(8,128)(2,1)S(1)} %constant_dynamic-update-slice_fusion.10.own), channel_id=1, source_target_pairs={{0,4},{1,5},{2,10},{3,11},{4,0},{5,1},{6,14},{7,15},{8,12},{9,13},... | collective-permute-start | bytes 2654216 | tf_op jit(solution)/shard_map/ppermute | solution.py:111
  160.0 1.6 collective-permute-start.37
  161.5 2.4 %shard_map.170 = f32[384,768]{1,0:T(8,128)} custom-call(s32[10]{0:T(128)S(1)} %stack.37.s, f32[384,768]{1,0:T(8,128)S(1)} %get-tuple-element.542.own, bf16[384,768]{1,0:T(8,128)(2,1)S(1)} %collective-permute-done.17.far, f32[384,768]{1,0:T(8,128)S(1)} %copy-done.6, f32[1,768]{1,0:T(1,128)S(1)} %broadcast_in_dim.16.gain, f32[384,768]{1,0:T(8,128)S(1)} %copy-done.10), custom_call_target="tpu_custom_call" | custom-call | flops 1 | bytes 1 | tf_op jit(solution)/shard_map/pallas_call | solution.py:54
  163.9 2.6 %shard_map.171 = (f32[2,2,8,384]{3,2,1,0:T(8,128)S(1)}, f32[3072,768]{1,0:T(8,128)}, f32[768,3072]{1,0:T(8,128)}) custom-call(s32[10]{0:T(128)S(1)} %stack.37.s, bf16[8,64,768]{2,1,0:T(8,128)(2,1)S(1)} %collective-permute-done.28.own, ...), custom_call_target="tpu_custom_call", output_to_operand_aliasing={{0}: (4, {}), {1}: (5, {}), {2}: (6, {})} | custom-call | flops 1 | bytes 1 | tf_op jit(solution)/shard_map/pallas_call | solution.py:54
  167.5 3.1 %shard_map.172 = (f32[2,2,8,384]{3,2,1,0:T(8,128)S(1)}, f32[3072,768]{1,0:T(8,128)}, f32[768,3072]{1,0:T(8,128)}, f32[768,768]{1,0:T(8,128)}) custom-call(s32[10]{0:T(128)S(1)} %stack.37.s, bf16[8,96,768]{2,1,0:T(8,128)(2,1)S(1)} %constant_dynamic-update-slice_fusion.8.own, ...), custom_call_target="tpu_custom_call", output_to_operand_aliasing={{0}: (4, {}), {1}: (5, {}), {2}: (6, {})} | custom-call | flops 1 | bytes 1 | tf_op jit(solution)/shard_map/pallas_call | solution.py:54
  170.6 2.4 %collective-permute-done.37 = bf16[4,64,768]{2,1,0:T(8,128)(2,1)S(1)} collective-permute-done((bf16[4,64,768]{2,1,0:T(8,128)(2,1)S(1)}, bf16[4,64,768]{2,1,0:T(8,128)(2,1)S(1)}, u32[]{:S(2)}, u32[]{:S(2)}) %collective-permute-start.37) | collective-permute-done | bytes 393248 | tf_op jit(solution)/shard_map/ppermute | solution.py:111
  174.7 3.1 %shard_map.173 = (f32[2,2,8,384]{3,2,1,0:T(8,128)S(1)}, f32[3072,768]{1,0:T(8,128)}, f32[768,3072]{1,0:T(8,128)}, f32[768,768]{1,0:T(8,128)}) custom-call(s32[10]{0:T(128)S(1)} %stack.37.s, bf16[8,96,768]{2,1,0:T(8,128)(2,1)S(1)} %collective-permute-done.39.own, ...), custom_call_target="tpu_custom_call", output_to_operand_aliasing={{0}: (4, {}), {1}: (5, {}), {2}: (6, {}), {3}: (7, {})} | custom-call | flops 1 | bytes 1 | tf_op jit(solution)/shard_map/pallas_call | solution.py:54
  177.8 3.2 %shard_map.174 = (f32[768,2304]{1,0:T(8,128)}, f32[8,8,96]{2,1,0:T(8,128)S(1)}) custom-call(s32[10]{0:T(128)S(1)} %stack.37.s, bf16[4,48,2304]{2,1,0:T(8,128)(2,1)S(1)} %constant_dynamic-update-slice_fusion.10.own, bf16[4,48,2304]{2,1,0:T(8,128)(2,1)S(1)} %collective-permute-done.41.other, bf16[768,2304]{1,0:T(8,128)(2,1)S(1)} %copy-done), custom_call_target="tpu_custom_call" | custom-call | flops 1 | bytes 1 | tf_op jit(solution)/shard_map/pallas_call | solution.py:54
  181.0 3.2 %shard_map.175 = (f32[768,2304]{1,0:T(8,128)}, f32[8,8,96]{2,1,0:T(8,128)S(1)}) custom-call(s32[10]{0:T(128)S(1)} %stack.37.s, bf16[4,48,2304]{2,1,0:T(8,128)(2,1)S(1)} %collective-permute-done.36.own, bf16[4,48,2304]{2,1,0:T(8,128)(2,1)S(1)} %collective-permute-done.40.other, ...), custom_call_target="tpu_custom_call", output_to_operand_aliasing={{0}: (4, {}), {1}: (5, {})} | custom-call | flops 1 | bytes 1 | tf_op jit(solution)/shard_map/pallas_call | solution.py:54
  185.2 2.6 %shard_map.176 = (f32[2,2,8,384]{3,2,1,0:T(8,128)S(1)}, f32[3072,768]{1,0:T(8,128)}, f32[768,3072]{1,0:T(8,128)}) custom-call(s32[10]{0:T(128)S(1)} %stack.37.s, bf16[8,64,768]{2,1,0:T(8,128)(2,1)S(1)} %constant_dynamic-update-slice_fusion.14.own, ...), custom_call_target="tpu_custom_call", output_to_operand_aliasing={{0}: (4, {}), {1}: (5, {}), {2}: (6, {})} | custom-call | flops 1 | bytes 1 | tf_op jit(solution)/shard_map/pallas_call | solution.py:54
  188.5 3.5 %shard_map.177 = (f32[2,2,8,384]{3,2,1,0:T(8,128)S(1)}, f32[3072,768]{1,0:T(8,128)}, f32[768,3072]{1,0:T(8,128)}) custom-call(s32[10]{0:T(128)S(1)} %stack.37.s, bf16[8,64,768]{2,1,0:T(8,128)(2,1)S(1)} %collective-permute-done.43.own, ...), custom_call_target="tpu_custom_call", output_to_operand_aliasing={{0}: (4, {}), {1}: (5, {}), {2}: (6, {})} | custom-call | flops 1 | bytes 1 | tf_op jit(solution)/shard_map/pallas_call | solution.py:54
  (161 shorter events, 25.4 us)
Async XLA Ops:
  0.6 18.2 %collective-permute-start = (bf16[384,768]{1,0:T(8,128)(2,1)}, bf16[384,768]{1,0:T(8,128)(2,1)}, u32[]{:S(2)}, u32[]{:S(2)}) collective-permute-start(bf16[384,768]{1,0:T(8,128)(2,1)} %bitcast.22), channel_id=1, source_target_pairs={{0,1},{1,0},{2,3},{3,2},{4,5},{5,4},{6,7},{7,6},{8,9},{9,8},{10,11... | collective-permute-start | bytes 1769480 | tf_op jit(solution)/shard_map/ppermute | solution.py:111
  3.7 13.7 %collective-permute-start.1 = (s32[1,384]{1,0:T(1,128)}, s32[1,384]{1,0:T(1,128)S(1)}, u32[]{:S(2)}, u32[]{:S(2)}) collective-permute-start(s32[1,384]{1,0:T(1,128)} %visible.1), channel_id=1, source_target_pairs={{0,1},{1,0},{2,3},{3,2},{4,5},{5,4},{6,7},{7,6},{8,9},{9,8},{10,11... | collective-permute-start | bytes 4616 | tf_op jit(solution)/shard_map/ppermute | solution.py:111
  11.0 18.4 %slice-start.2 = ((s8[4718592]{0:T(1024)(128)(4,1)}), s8[4194304]{0:T(1024)(128)(4,1)S(1)}, s32[]{:S(2)}) async-start(s8[4718592]{0:T(1024)(128)(4,1)} %bitcast.14), calls=%async_computation.2 | async-start | bytes 8388608
  28.7 18.6 %copy-start.3 = (bf16[1152,384]{1,0:T(8,128)(2,1)}, bf16[1152,384]{1,0:T(8,128)(2,1)S(1)}, u32[]{:S(2)}) copy-start(bf16[1152,384]{1,0:T(8,128)(2,1)S(1)} %get-tuple-element.413.nt) | copy-start | bytes 2654212
  28.8 5.3 %collective-permute-start.3 = (bf16[1152,384]{1,0:T(8,128)(2,1)S(1)}, bf16[1152,384]{1,0:T(8,128)(2,1)S(1)}, u32[]{:S(2)}, u32[]{:S(2)}) collective-permute-start(bf16[1152,384]{1,0:T(8,128)(2,1)S(1)} %get-tuple-element.413.nt), channel_id=1, source_target_pairs={{0,2},{1,3},{2,0},{3,1},{4,6},{5,7},{6,4},{7,5},{8,10},{9,11},{10,... | collective-permute-start | bytes 2654216 | tf_op jit(solution)/shard_map/ppermute | solution.py:111
  28.9 5.2 %collective-permute-start.2 = (bf16[384,768]{1,0:T(8,128)(2,1)S(1)}, bf16[384,768]{1,0:T(8,128)(2,1)S(1)}, u32[]{:S(2)}, u32[]{:S(2)}) collective-permute-start(bf16[384,768]{1,0:T(8,128)(2,1)S(1)} %bitcast.16), channel_id=1, source_target_pairs={{0,2},{1,3},{2,0},{3,1},{4,6},{5,7},{6,4},{7,5},{8,10},{9,11},{10,... | collective-permute-start | bytes 1769480 | tf_op jit(solution)/shard_map/ppermute | solution.py:111
  33.9 13.4 %collective-permute-start.4 = (bf16[2,384,512]{2,1,0:T(8,128)(2,1)S(1)}, bf16[2,384,512]{2,1,0:T(8,128)(2,1)S(1)}, u32[]{:S(2)}, u32[]{:S(2)}) collective-permute-start(bf16[2,384,512]{2,1,0:T(8,128)(2,1)S(1)} %get-tuple-element.367), channel_id=1, source_target_pairs={{0,2},{1,3},{2,0},{3,1},{4,6},{5,7},{6,4},{7,5},{8,10},{9,11},{10,... | collective-permute-start | bytes 2359304 | tf_op jit(solution)/shard_map/ppermute | solution.py:111
  45.0 14.6 %collective-permute-start.7 = (bf16[2,384,512]{2,1,0:T(8,128)(2,1)S(1)}, bf16[2,384,512]{2,1,0:T(8,128)(2,1)S(1)}, u32[]{:S(2)}, u32[]{:S(2)}) collective-permute-start(bf16[2,384,512]{2,1,0:T(8,128)(2,1)S(1)} %get-tuple-element.389), channel_id=1, source_target_pairs={{0,2},{1,3},{2,0},{3,1},{4,6},{5,7},{6,4},{7,5},{8,10},{9,11},{10,... | collective-permute-start | bytes 2359304 | tf_op jit(solution)/shard_map/ppermute | solution.py:111
  45.4 14.2 %collective-permute-start.8 = (bf16[384,768]{1,0:T(8,128)(2,1)S(1)}, bf16[384,768]{1,0:T(8,128)(2,1)S(1)}, u32[]{:S(2)}, u32[]{:S(2)}) collective-permute-start(bf16[384,768]{1,0:T(8,128)(2,1)S(1)} %get-tuple-element.405.refs_2_), channel_id=1, source_target_pairs={{0,2},{1,3},{2,0},{3,1},{4,6},{5,7},{6,4},{7,5},{8,10},{9,11},{10,... | collective-permute-start | bytes 1769480 | tf_op jit(solution)/shard_map/ppermute | solution.py:111
  45.5 14.1 %collective-permute-start.9 = (bf16[384,384]{1,0:T(8,128)(2,1)S(1)}, bf16[384,384]{1,0:T(8,128)(2,1)S(1)}, u32[]{:S(2)}, u32[]{:S(2)}) collective-permute-start(bf16[384,384]{1,0:T(8,128)(2,1)S(1)} %get-tuple-element.395), channel_id=1, source_target_pairs={{0,1},{1,0},{2,3},{3,2},{4,5},{5,4},{6,7},{7,6},{8,9},{9,8},{10,11... | collective-permute-start | bytes 884744 | tf_op jit(solution)/shard_map/ppermute | solution.py:111
  47.2 16.5 %collective-permute-start.6 = (bf16[2,384,512]{2,1,0:T(8,128)(2,1)S(1)}, bf16[2,384,512]{2,1,0:T(8,128)(2,1)S(1)}, u32[]{:S(2)}, u32[]{:S(2)}) collective-permute-start(bf16[2,384,512]{2,1,0:T(8,128)(2,1)S(1)} %get-tuple-element.386), channel_id=1, source_target_pairs={{0,2},{1,3},{2,0},{3,1},{4,6},{5,7},{6,4},{7,5},{8,10},{9,11},{10,... | collective-permute-start | bytes 2359304 | tf_op jit(solution)/shard_map/ppermute | solution.py:111
  50.1 17.8 %collective-permute-start.5 = (bf16[8,64,768]{2,1,0:T(8,128)(2,1)S(1)}, bf16[8,64,768]{2,1,0:T(8,128)(2,1)S(1)}, u32[]{:S(2)}, u32[]{:S(2)}) collective-permute-start(bf16[8,64,768]{2,1,0:T(8,128)(2,1)S(1)} %get-tuple-element.384), channel_id=1, source_target_pairs={{0,4},{1,5},{2,3},{3,2},{4,0},{5,1},{6,7},{7,6},{8,12},{9,13},{10,... | collective-permute-start | bytes 2359304 | tf_op jit(solution)/shard_map/ppermute | solution.py:111
  63.1 16.3 %collective-permute-start.10 = (bf16[8,96,768]{2,1,0:T(8,128)(2,1)S(1)}, bf16[8,96,768]{2,1,0:T(8,128)(2,1)S(1)}, u32[]{:S(2)}, u32[]{:S(2)}) collective-permute-start(bf16[8,96,768]{2,1,0:T(8,128)(2,1)S(1)} %get-tuple-element.434), channel_id=1, source_target_pairs={{0,1},{1,0},{2,6},{3,7},{4,5},{5,4},{6,2},{7,3},{8,9},{9,8},{10,14... | collective-permute-start | bytes 3538952 | tf_op jit(solution)/shard_map/ppermute | solution.py:111
  66.2 23.4 %collective-permute-start.16 = (bf16[8,64,768]{2,1,0:T(8,128)(2,1)S(1)}, bf16[8,64,768]{2,1,0:T(8,128)(2,1)S(1)}, u32[]{:S(2)}, u32[]{:S(2)}) collective-permute-start(bf16[8,64,768]{2,1,0:T(8,128)(2,1)S(1)} %get-tuple-element.461), channel_id=1, source_target_pairs={{0,8},{1,9},{2,6},{3,7},{4,12},{5,13},{6,2},{7,3},{8,0},{9,1},{10,... | collective-permute-start | bytes 2359304 | tf_op jit(solution)/shard_map/ppermute | solution.py:111
  69.1 17.3 %collective-permute-start.12 = (bf16[4,64,768]{2,1,0:T(8,128)(2,1)S(1)}, bf16[4,64,768]{2,1,0:T(8,128)(2,1)S(1)}, u32[]{:S(2)}, u32[]{:S(2)}) collective-permute-start(bf16[4,64,768]{2,1,0:T(8,128)(2,1)S(1)} %add_convert_fusion.7), channel_id=1, source_target_pairs={{0,1},{1,0},{2,10},{3,11},{4,5},{5,4},{6,14},{7,15},{8,9},{9,8},{1... | collective-permute-start | bytes 1179656 | tf_op jit(solution)/shard_map/ppermute | solution.py:111
  79.5 9.9 %collective-permute-start.11 = (bf16[4,96,768]{2,1,0:T(8,128)(2,1)S(1)}, bf16[4,96,768]{2,1,0:T(8,128)(2,1)S(1)}, u32[]{:S(2)}, u32[]{:S(2)}) collective-permute-start(bf16[4,96,768]{2,1,0:T(8,128)(2,1)S(1)} %add_convert_fusion.1), channel_id=1, source_target_pairs={{0,8},{1,9},{2,3},{3,2},{4,12},{5,13},{6,7},{7,6},{8,0},{9,1},{10,... | collective-permute-start | bytes 1769480 | tf_op jit(solution)/shard_map/ppermute | solution.py:111
  86.4 5.7 %collective-permute-start.15 = (bf16[2,64,768]{2,1,0:T(8,128)(2,1)S(1)}, bf16[2,64,768]{2,1,0:T(8,128)(2,1)S(1)}, u32[]{:S(2)}, u32[]{:S(2)}) collective-permute-start(bf16[2,64,768]{2,1,0:T(8,128)(2,1)S(1)} %add_convert_fusion.23), channel_id=1, source_target_pairs={{0,8},{1,9},{2,6},{3,7},{4,12},{5,13},{6,2},{7,3},{8,0},{9,1},{10,... | collective-permute-start | bytes 589832 | tf_op jit(solution)/shard_map/ppermute | solution.py:111
  88.3 7.3 %collective-permute-start.14 = (bf16[8,48,1152]{2,1,0:T(8,128)(2,1)S(1)}, bf16[8,48,1152]{2,1,0:T(8,128)(2,1)S(1)}, u32[]{:S(2)}, u32[]{:S(2)}) collective-permute-start(bf16[8,48,1152]{2,1,0:T(8,128)(2,1)S(1)} %get-tuple-element.458), channel_id=1, source_target_pairs={{0,2},{1,3},{2,0},{3,1},{4,6},{5,7},{6,4},{7,5},{8,10},{9,11},{10,... | collective-permute-start | bytes 2654216 | tf_op jit(solution)/shard_map/ppermute | solution.py:111
  92.2 6.7 %collective-permute-start.13 = (bf16[2,96,768]{2,1,0:T(8,128)(2,1)S(1)}, bf16[2,96,768]{2,1,0:T(8,128)(2,1)S(1)}, u32[]{:S(2)}, u32[]{:S(2)}) collective-permute-start(bf16[2,96,768]{2,1,0:T(8,128)(2,1)S(1)} %add_convert_fusion.11), channel_id=1, source_target_pairs={{0,4},{1,5},{2,10},{3,11},{4,0},{5,1},{6,14},{7,15},{8,12},{9,13},... | collective-permute-start | bytes 884744 | tf_op jit(solution)/shard_map/ppermute | solution.py:111
  92.2 12.4 %collective-permute-start.19 = (bf16[4,64,768]{2,1,0:T(8,128)(2,1)S(1)}, bf16[4,64,768]{2,1,0:T(8,128)(2,1)S(1)}, u32[]{:S(2)}, u32[]{:S(2)}) collective-permute-start(bf16[4,64,768]{2,1,0:T(8,128)(2,1)S(1)} %add_convert_fusion.5), channel_id=1, source_target_pairs={{0,1},{1,0},{2,3},{3,2},{4,5},{5,4},{6,7},{7,6},{8,9},{9,8},{10,11... | collective-permute-start | bytes 1179656 | tf_op jit(solution)/shard_map/ppermute | solution.py:111
  93.0 11.7 %collective-permute-start.18 = (bf16[2,64,768]{2,1,0:T(8,128)(2,1)S(1)}, bf16[2,64,768]{2,1,0:T(8,128)(2,1)S(1)}, u32[]{:S(2)}, u32[]{:S(2)}) collective-permute-start(bf16[2,64,768]{2,1,0:T(8,128)(2,1)S(1)} %add_convert_fusion.21), channel_id=1, source_target_pairs={{0,16},{1,17},{2,18},{3,19},{4,20},{5,21},{6,22},{7,23},{8,24},{9,... | collective-permute-start | bytes 589832 | tf_op jit(solution)/shard_map/ppermute | solution.py:111
  95.8 8.7 %collective-permute-start.20 = (bf16[4,48,1152]{2,1,0:T(8,128)(2,1)S(1)}, bf16[4,48,1152]{2,1,0:T(8,128)(2,1)S(1)}, u32[]{:S(2)}, u32[]{:S(2)}) collective-permute-start(bf16[4,48,1152]{2,1,0:T(8,128)(2,1)S(1)} %add_convert_fusion.3), channel_id=1, source_target_pairs={{0,4},{1,5},{2,10},{3,11},{4,0},{5,1},{6,14},{7,15},{8,12},{9,13},... | collective-permute-start | bytes 1327112 | tf_op jit(solution)/shard_map/ppermute | solution.py:111
  101.6 14.9 %collective-permute-start.17 = (bf16[384,768]{1,0:T(8,128)(2,1)S(1)}, bf16[384,768]{1,0:T(8,128)(2,1)S(1)}, u32[]{:S(2)}, u32[]{:S(2)}) collective-permute-start(bf16[384,768]{1,0:T(8,128)(2,1)S(1)} %get-tuple-element.481), channel_id=1, source_target_pairs={{0,1},{1,0},{2,3},{3,2},{4,5},{5,4},{6,7},{7,6},{8,9},{9,8},{10,11... | collective-permute-start | bytes 1769480 | tf_op jit(solution)/shard_map/ppermute | solution.py:111
  102.0 21.7 %collective-permute-start.22 = (bf16[2,96,768]{2,1,0:T(8,128)(2,1)S(1)}, bf16[2,96,768]{2,1,0:T(8,128)(2,1)S(1)}, u32[]{:S(2)}, u32[]{:S(2)}) collective-permute-start(bf16[2,96,768]{2,1,0:T(8,128)(2,1)S(1)} %add_convert_fusion.9), channel_id=1, source_target_pairs={{0,16},{1,17},{2,18},{3,19},{4,20},{5,21},{6,22},{7,23},{8,24},{9,... | collective-permute-start | bytes 884744 | tf_op jit(solution)/shard_map/ppermute | solution.py:111
  104.8 19.5 %collective-permute-start.21 = (bf16[2,64,768]{2,1,0:T(8,128)(2,1)S(1)}, bf16[2,64,768]{2,1,0:T(8,128)(2,1)S(1)}, u32[]{:S(2)}, u32[]{:S(2)}) collective-permute-start(bf16[2,64,768]{2,1,0:T(8,128)(2,1)S(1)} %add_convert_fusion.18), channel_id=1, source_target_pairs={{0,8},{1,9},{2,6},{3,7},{4,12},{5,13},{6,2},{7,3},{8,0},{9,1},{10,... | collective-permute-start | bytes 589832 | tf_op jit(solution)/shard_map/ppermute | solution.py:111
  106.6 19.0 %collective-permute-start.24 = (bf16[2,48,1152]{2,1,0:T(8,128)(2,1)S(1)}, bf16[2,48,1152]{2,1,0:T(8,128)(2,1)S(1)}, u32[]{:S(2)}, u32[]{:S(2)}) collective-permute-start(bf16[2,48,1152]{2,1,0:T(8,128)(2,1)S(1)} %add_convert_fusion.15), channel_id=1, source_target_pairs={{0,8},{1,9},{2,18},{3,19},{4,12},{5,13},{6,22},{7,23},{8,0},{9,1},... | collective-permute-start | bytes 663560 | tf_op jit(solution)/shard_map/ppermute | solution.py:111
  106.9 25.6 %collective-permute-start.26 = (bf16[2,64,768]{2,1,0:T(8,128)(2,1)S(1)}, bf16[2,64,768]{2,1,0:T(8,128)(2,1)S(1)}, u32[]{:S(2)}, u32[]{:S(2)}) collective-permute-start(bf16[2,64,768]{2,1,0:T(8,128)(2,1)S(1)} %add_convert_fusion.20), channel_id=1, source_target_pairs={{0,4},{1,5},{2,18},{3,19},{4,0},{5,1},{6,22},{7,23},{8,12},{9,13},... | collective-permute-start | bytes 589832 | tf_op jit(solution)/shard_map/ppermute | solution.py:111
  123.8 8.7 %collective-permute-start.27 = (bf16[2,96,768]{2,1,0:T(8,128)(2,1)S(1)}, bf16[2,96,768]{2,1,0:T(8,128)(2,1)S(1)}, u32[]{:S(2)}, u32[]{:S(2)}) collective-permute-start(bf16[2,96,768]{2,1,0:T(8,128)(2,1)S(1)} %add_convert_fusion.8), channel_id=1, source_target_pairs={{0,4},{1,5},{2,10},{3,11},{4,0},{5,1},{6,14},{7,15},{8,12},{9,13},... | collective-permute-start | bytes 884744 | tf_op jit(solution)/shard_map/ppermute | solution.py:111
  124.3 12.4 %collective-permute-start.23 = (bf16[4,64,768]{2,1,0:T(8,128)(2,1)S(1)}, bf16[4,64,768]{2,1,0:T(8,128)(2,1)S(1)}, u32[]{:S(2)}, u32[]{:S(2)}) collective-permute-start(bf16[4,64,768]{2,1,0:T(8,128)(2,1)S(1)} %constant_dynamic-update-slice_fusion), channel_id=1, source_target_pairs={{0,1},{1,0},{2,10},{3,11},{4,5},{5,4},{6,14},{7,15},{8,9},{9,8},{1... | collective-permute-start | bytes 1179656 | tf_op jit(solution)/shard_map/ppermute | solution.py:111
  125.6 10.0 %collective-permute-start.25 = (bf16[2,48,1152]{2,1,0:T(8,128)(2,1)S(1)}, bf16[2,48,1152]{2,1,0:T(8,128)(2,1)S(1)}, u32[]{:S(2)}, u32[]{:S(2)}) collective-permute-start(bf16[2,48,1152]{2,1,0:T(8,128)(2,1)S(1)} %add_convert_fusion.13), channel_id=1, source_target_pairs={{0,16},{1,17},{2,6},{3,7},{4,20},{5,21},{6,2},{7,3},{8,24},{9,25},... | collective-permute-start | bytes 663560 | tf_op jit(solution)/shard_map/ppermute | solution.py:111
  132.5 14.2 %collective-permute-start.31 = (bf16[4,96,768]{2,1,0:T(8,128)(2,1)S(1)}, bf16[4,96,768]{2,1,0:T(8,128)(2,1)S(1)}, u32[]{:S(2)}, u32[]{:S(2)}) collective-permute-start(bf16[4,96,768]{2,1,0:T(8,128)(2,1)S(1)} %constant_dynamic-update-slice_fusion.2), channel_id=1, source_target_pairs={{0,8},{1,9},{2,3},{3,2},{4,12},{5,13},{6,7},{7,6},{8,0},{9,1},{10,... | collective-permute-start | bytes 1769480 | tf_op jit(solution)/shard_map/ppermute | solution.py:111
  132.7 15.8 %collective-permute-start.30 = (bf16[2,64,768]{2,1,0:T(8,128)(2,1)S(1)}, bf16[2,64,768]{2,1,0:T(8,128)(2,1)S(1)}, u32[]{:S(2)}, u32[]{:S(2)}) collective-permute-start(bf16[2,64,768]{2,1,0:T(8,128)(2,1)S(1)} %add_convert_fusion.17), channel_id=1, source_target_pairs={{0,16},{1,17},{2,10},{3,11},{4,20},{5,21},{6,14},{7,15},{8,24},{9,... | collective-permute-start | bytes 589832 | tf_op jit(solution)/shard_map/ppermute | solution.py:111
  135.7 8.4 %collective-permute-start.32 = (bf16[2,48,1152]{2,1,0:T(8,128)(2,1)S(1)}, bf16[2,48,1152]{2,1,0:T(8,128)(2,1)S(1)}, u32[]{:S(2)}, u32[]{:S(2)}) collective-permute-start(bf16[2,48,1152]{2,1,0:T(8,128)(2,1)S(1)} %add_convert_fusion.12), channel_id=1, source_target_pairs={{0,1},{1,0},{2,3},{3,2},{4,5},{5,4},{6,7},{7,6},{8,9},{9,8},{10,11... | collective-permute-start | bytes 663560 | tf_op jit(solution)/shard_map/ppermute | solution.py:111
  136.8 11.7 %collective-permute-start.29 = (bf16[8,64,768]{2,1,0:T(8,128)(2,1)S(1)}, bf16[8,64,768]{2,1,0:T(8,128)(2,1)S(1)}, u32[]{:S(2)}, u32[]{:S(2)}) collective-permute-start(bf16[8,64,768]{2,1,0:T(8,128)(2,1)S(1)} %constant_dynamic-update-slice_fusion.4.own), channel_id=1, source_target_pairs={{0,2},{1,3},{2,0},{3,1},{4,6},{5,7},{6,4},{7,5},{8,10},{9,11},{10,... | collective-permute-start | bytes 2359304 | tf_op jit(solution)/shard_map/ppermute | solution.py:111
  136.9 14.0 %collective-permute-start.28 = (bf16[8,64,768]{2,1,0:T(8,128)(2,1)S(1)}, bf16[8,64,768]{2,1,0:T(8,128)(2,1)S(1)}, u32[]{:S(2)}, u32[]{:S(2)}) collective-permute-start(bf16[8,64,768]{2,1,0:T(8,128)(2,1)S(1)} %constant_dynamic-update-slice_fusion.4.own), channel_id=1, source_target_pairs={{0,4},{1,5},{2,3},{3,2},{4,0},{5,1},{6,7},{7,6},{8,12},{9,13},{10,... | collective-permute-start | bytes 2359304 | tf_op jit(solution)/shard_map/ppermute | solution.py:111
  144.2 12.9 %collective-permute-start.35 = (bf16[2,48,2304]{2,1,0:T(8,128)(2,1)S(1)}, bf16[2,48,2304]{2,1,0:T(8,128)(2,1)S(1)}, u32[]{:S(2)}, u32[]{:S(2)}) collective-permute-start(bf16[2,48,2304]{2,1,0:T(8,128)(2,1)S(1)} %constant_dynamic-update-slice_fusion.6), channel_id=1, source_target_pairs={{0,8},{1,9},{2,18},{3,19},{4,12},{5,13},{6,22},{7,23},{8,0},{9,1},... | collective-permute-start | bytes 1327112 | tf_op jit(solution)/shard_map/ppermute | solution.py:111
  146.8 19.8 %collective-permute-start.39 = (bf16[8,96,768]{2,1,0:T(8,128)(2,1)S(1)}, bf16[8,96,768]{2,1,0:T(8,128)(2,1)S(1)}, u32[]{:S(2)}, u32[]{:S(2)}) collective-permute-start(bf16[8,96,768]{2,1,0:T(8,128)(2,1)S(1)} %constant_dynamic-update-slice_fusion.8.own), channel_id=1, source_target_pairs={{0,1},{1,0},{2,6},{3,7},{4,5},{5,4},{6,2},{7,3},{8,9},{9,8},{10,14... | collective-permute-start | bytes 3538952 | tf_op jit(solution)/shard_map/ppermute | solution.py:111
  148.5 19.0 %collective-permute-start.38 = (bf16[8,96,768]{2,1,0:T(8,128)(2,1)S(1)}, bf16[8,96,768]{2,1,0:T(8,128)(2,1)S(1)}, u32[]{:S(2)}, u32[]{:S(2)}) collective-permute-start(bf16[8,96,768]{2,1,0:T(8,128)(2,1)S(1)} %constant_dynamic-update-slice_fusion.8.own), channel_id=1, source_target_pairs={{0,2},{1,3},{2,0},{3,1},{4,6},{5,7},{6,4},{7,5},{8,10},{9,11},{10,... | collective-permute-start | bytes 3538952 | tf_op jit(solution)/shard_map/ppermute | solution.py:111
  148.5 11.4 %collective-permute-start.34 = (bf16[2,64,768]{2,1,0:T(8,128)(2,1)S(1)}, bf16[2,64,768]{2,1,0:T(8,128)(2,1)S(1)}, u32[]{:S(2)}, u32[]{:S(2)}) collective-permute-start(bf16[2,64,768]{2,1,0:T(8,128)(2,1)S(1)} %add_convert_fusion.16), channel_id=1, source_target_pairs={{0,4},{1,5},{2,18},{3,19},{4,0},{5,1},{6,22},{7,23},{8,12},{9,13},... | collective-permute-start | bytes 589832 | tf_op jit(solution)/shard_map/ppermute | solution.py:111
  157.1 4.4 %collective-permute-start.33 = (bf16[8,64,768]{2,1,0:T(8,128)(2,1)S(1)}, bf16[8,64,768]{2,1,0:T(8,128)(2,1)S(1)}, u32[]{:S(2)}, u32[]{:S(2)}) collective-permute-start(bf16[8,64,768]{2,1,0:T(8,128)(2,1)S(1)} %collective-permute-done.28.own), channel_id=1, source_target_pairs={{0,2},{1,3},{2,0},{3,1},{4,6},{5,7},{6,4},{7,5},{8,10},{9,11},{10,... | collective-permute-start | bytes 2359304 | tf_op jit(solution)/shard_map/ppermute | solution.py:111
  157.2 16.0 %collective-permute-start.36 = (bf16[4,48,2304]{2,1,0:T(8,128)(2,1)S(1)}, bf16[4,48,2304]{2,1,0:T(8,128)(2,1)S(1)}, u32[]{:S(2)}, u32[]{:S(2)}) collective-permute-start(bf16[4,48,2304]{2,1,0:T(8,128)(2,1)S(1)} %constant_dynamic-update-slice_fusion.10.own), channel_id=1, source_target_pairs={{0,4},{1,5},{2,10},{3,11},{4,0},{5,1},{6,14},{7,15},{8,12},{9,13},... | collective-permute-start | bytes 2654216 | tf_op jit(solution)/shard_map/ppermute | solution.py:111
  160.0 13.0 %collective-permute-start.37 = (bf16[4,64,768]{2,1,0:T(8,128)(2,1)S(1)}, bf16[4,64,768]{2,1,0:T(8,128)(2,1)S(1)}, u32[]{:S(2)}, u32[]{:S(2)}) collective-permute-start(bf16[4,64,768]{2,1,0:T(8,128)(2,1)S(1)} %constant_dynamic-update-slice_fusion.12), channel_id=1, source_target_pairs={{0,1},{1,0},{2,3},{3,2},{4,5},{5,4},{6,7},{7,6},{8,9},{9,8},{10,11... | collective-permute-start | bytes 1179656 | tf_op jit(solution)/shard_map/ppermute | solution.py:111
  166.5 8.1 %collective-permute-start.42 = (bf16[8,96,768]{2,1,0:T(8,128)(2,1)S(1)}, bf16[8,96,768]{2,1,0:T(8,128)(2,1)S(1)}, u32[]{:S(2)}, u32[]{:S(2)}) collective-permute-start(bf16[8,96,768]{2,1,0:T(8,128)(2,1)S(1)} %collective-permute-done.39.own), channel_id=1, source_target_pairs={{0,2},{1,3},{2,0},{3,1},{4,6},{5,7},{6,4},{7,5},{8,10},{9,11},{10,... | collective-permute-start | bytes 3538952 | tf_op jit(solution)/shard_map/ppermute | solution.py:111
  167.4 7.3 %collective-permute-start.41 = (bf16[4,48,2304]{2,1,0:T(8,128)(2,1)S(1)}, bf16[4,48,2304]{2,1,0:T(8,128)(2,1)S(1)}, u32[]{:S(2)}, u32[]{:S(2)}) collective-permute-start(bf16[4,48,2304]{2,1,0:T(8,128)(2,1)S(1)} %constant_dynamic-update-slice_fusion.10.own), channel_id=1, source_target_pairs={{0,2},{1,3},{2,0},{3,1},{4,6},{5,7},{6,4},{7,5},{8,10},{9,11},{10,... | collective-permute-start | bytes 2654216 | tf_op jit(solution)/shard_map/ppermute | solution.py:111
  173.2 7.8 %collective-permute-start.40 = (bf16[4,48,2304]{2,1,0:T(8,128)(2,1)S(1)}, bf16[4,48,2304]{2,1,0:T(8,128)(2,1)S(1)}, u32[]{:S(2)}, u32[]{:S(2)}) collective-permute-start(bf16[4,48,2304]{2,1,0:T(8,128)(2,1)S(1)} %collective-permute-done.36.own), channel_id=1, source_target_pairs={{0,2},{1,3},{2,0},{3,1},{4,6},{5,7},{6,4},{7,5},{8,10},{9,11},{10,... | collective-permute-start | bytes 2654216 | tf_op jit(solution)/shard_map/ppermute | solution.py:111
  173.2 12.0 %collective-permute-start.43 = (bf16[8,64,768]{2,1,0:T(8,128)(2,1)S(1)}, bf16[8,64,768]{2,1,0:T(8,128)(2,1)S(1)}, u32[]{:S(2)}, u32[]{:S(2)}) collective-permute-start(bf16[8,64,768]{2,1,0:T(8,128)(2,1)S(1)} %constant_dynamic-update-slice_fusion.14.own), channel_id=1, source_target_pairs={{0,8},{1,9},{2,6},{3,7},{4,12},{5,13},{6,2},{7,3},{8,0},{9,1},{10,... | collective-permute-start | bytes 2359304 | tf_op jit(solution)/shard_map/ppermute | solution.py:111
  173.7 11.5 %collective-permute-start.45 = (bf16[8,64,768]{2,1,0:T(8,128)(2,1)S(1)}, bf16[8,64,768]{2,1,0:T(8,128)(2,1)S(1)}, u32[]{:S(2)}, u32[]{:S(2)}) collective-permute-start(bf16[8,64,768]{2,1,0:T(8,128)(2,1)S(1)} %constant_dynamic-update-slice_fusion.14.own), channel_id=1, source_target_pairs={{0,2},{1,3},{2,0},{3,1},{4,6},{5,7},{6,4},{7,5},{8,10},{9,11},{10,... | collective-permute-start | bytes 2359304 | tf_op jit(solution)/shard_map/ppermute | solution.py:111
  185.2 3.3 %collective-permute-start.44 = (bf16[8,64,768]{2,1,0:T(8,128)(2,1)S(1)}, bf16[8,64,768]{2,1,0:T(8,128)(2,1)S(1)}, u32[]{:S(2)}, u32[]{:S(2)}) collective-permute-start(bf16[8,64,768]{2,1,0:T(8,128)(2,1)S(1)} %collective-permute-done.43.own), channel_id=1, source_target_pairs={{0,2},{1,3},{2,0},{3,1},{4,6},{5,7},{6,4},{7,5},{8,10},{9,11},{10,... | collective-permute-start | bytes 2359304 | tf_op jit(solution)/shard_map/ppermute | solution.py:111
  (17 other events, 100.4 us)
